TPU v7x, 32 devices: a whole 2x2x4 slice. The times are simulated.
32 devices in a mesh: groups: 2 (over y), frames: 4 (over z), rows: 4 (over x, core).
Axes of the slice: x: 2, y: 2, z: 4, core: 2. Of those that a mesh axis runs over, the one named last changes fastest.
Arguments:
- latents: bfloat16 [16, 8, 16, 1280], P('rows', ('groups', 'frames')), parts along dimension 1, may hold values from -6 to 6
- spatial_weight: bfloat16 [3, 3, 1280, 1280], P(None, None, None, 'rows'), may hold values from -0.0546875 to 0.0546875
- spatial_bias: float32 [1280], P('rows'), may hold values from -3 to 3
- norm_gain: float32 [1280], P('rows'), may hold values from 0.1 to 1.9
- norm_shift: float32 [1280], P('rows'), may hold values from -3 to 3
- temporal_weight: bfloat16 [3, 1280, 1280], P(None, 'rows'), may hold values from -0.09375 to 0.09375
- temporal_bias: float32 [1280], replicated, may hold values from -3 to 3
- token_gain: float32 [1280], replicated, may hold values from 0.1 to 1.9
- query_weight: bfloat16 [1280, 1024], P(None, 'rows'), may hold values from -4 to 4
- key_weight: bfloat16 [1280, 1024], P(None, 'rows'), may hold values from -4 to 4
- value_weight: bfloat16 [1280, 1024], P(None, 'rows'), may hold values from -0.15625 to 0.15625
- output_weight: bfloat16 [1024, 1280], P('rows'), may hold values from -0.1875 to 0.1875
Outputs:
- denoised: bfloat16 [16, 8, 16, 1280], P('rows', ('groups', 'frames')), parts along dimension 1
There are 2 independent parts, one for each index of `groups`. A program takes and returns all parts, laid end to end along the dimension named above; an argument that names none is the same for every part. Nothing has to cross between parts.
All inputs are finite; a program needn't handle non-finite values.
Results may differ from a plain program's by a relative error of at most 0.034.
Values may be sent and summed in bfloat16 or wider, within the bound.
No kernel may reach another device: no remote copies, remote signals or barrier semaphores. Data moves between devices by JAX's collectives and lax.ppermute only.
A program may use at most 128 MiB of HBM per device.

v0:
```python
import math

import jax
import jax.numpy as jnp
from jax import lax
from jax.sharding import PartitionSpec as P

HD = 64
NORM_GROUPS = 32


def padded_2(array, sides, width):
    for axis, dim in sides:
        peers, length = (lax.axis_size(axis), array.shape[dim])
        up = [(i, (i + 1) % peers) for i in range(peers - 1)]
        down = [(j, i) for i, j in up]
        last = lax.slice_in_dim(array, length - width, length, axis=dim)
        leading = lax.slice_in_dim(array, 0, width, axis=dim)
        before = lax.ppermute(last, axis, up)
        after = lax.ppermute(leading, axis, down)
        array = jnp.concatenate([before, array, after], axis=dim)
    return array


def shifted_2(value, axis, steps):
    count = lax.axis_size(axis)
    pairs = [(source, (source + steps) % count) for source in range(count)]
    return lax.ppermute(value, axis, pairs)


def conv_plane(field, weight, bias):
    rows_n, frames_n, cols_n, chans = field.shape
    padded = jnp.pad(field, ((1, 1), (0, 0), (1, 1), (0, 0)))
    total = jnp.zeros((rows_n * frames_n * cols_n, weight.shape[3]), jnp.float32)
    for row_off in range(3):
        for col_off in range(3):
            window = padded[row_off : row_off + rows_n, :, col_off : col_off + cols_n, :].reshape(
                -1, chans
            )
            total = total + jnp.dot(
                window, weight[row_off, col_off], preferred_element_type=jnp.float32
            )
    return total.reshape(rows_n, frames_n, cols_n, -1) + bias


def layer_norm(field, token_gain):
    flat = field.astype(jnp.float32)
    token_mean = jnp.mean(flat, axis=-1, keepdims=True)
    shifted = flat - token_mean
    token_var = jnp.mean(shifted * shifted, axis=-1, keepdims=True)
    return (shifted / jnp.sqrt(token_var + 1e-05) * token_gain).astype(jnp.bfloat16)


def attend(queries, carried, keys, values):
    block = queries.shape[0]
    head_count = queries.shape[1]
    block_count = keys.shape[0] // block
    key_blocks = keys.reshape(block_count, block, head_count, HD)
    value_blocks = values.reshape(block_count, block, head_count, HD)
    scale = 1.0 / math.sqrt(HD)

    def visit_block(state, block_pair):
        running_max, denominator, numerator = state
        key_block, value_block = block_pair
        scores = (
            jnp.einsum("qhd,khd->qhk", queries, key_block, preferred_element_type=jnp.float32)
            * scale
        )
        new_max = jnp.maximum(running_max, jnp.max(scores, axis=-1))
        shrink = jnp.exp(running_max - new_max)
        weights = jnp.exp(scores - new_max[..., None])
        denominator = denominator * shrink + jnp.sum(weights, axis=-1)
        numerator = numerator * shrink[..., None] + jnp.einsum(
            "qhk,khd->qhd",
            weights.astype(jnp.bfloat16),
            value_block,
            preferred_element_type=jnp.float32,
        )
        return ((new_max, denominator, numerator), None)

    result, _ = lax.scan(visit_block, carried, (key_blocks, value_blocks))
    return result


def body(
    latents,
    spatial_weight,
    spatial_bias,
    norm_gain,
    norm_shift,
    temporal_weight,
    temporal_bias,
    token_gain,
    query_weight,
    key_weight,
    value_weight,
    output_weight,
):
    row_count, frame_count, width_cells, channels = latents.shape
    plane = lax.all_gather(latents, "rows", axis=0, tiled=True)
    plane_rows = plane.shape[0]
    local_out = spatial_weight.shape[3]
    spatial = conv_plane(plane, spatial_weight, spatial_bias)
    local_groups = NORM_GROUPS // lax.axis_size("rows")
    grouped = spatial.reshape(plane_rows, frame_count, width_cells, local_groups, -1)
    group_mean = jnp.mean(grouped, axis=(0, 2, 4), keepdims=True)
    centred = grouped - group_mean
    group_var = jnp.mean(centred * centred, axis=(0, 2, 4), keepdims=True)
    scaled = (centred / jnp.sqrt(group_var + 1e-05)).reshape(
        plane_rows, frame_count, width_cells, local_out
    ) * norm_gain + norm_shift
    activated = jax.nn.silu(scaled).astype(jnp.bfloat16)
    rim = padded_2(activated, (("frames", 1),), 1)
    row_total = row_count * lax.axis_size("rows")
    row_piece = rim
    total = jnp.zeros((row_total * frame_count * width_cells, channels), jnp.float32)
    for lag_index in range(3):
        window = row_piece[:, lag_index : lag_index + frame_count].reshape(-1, local_out)
        total = total + jnp.dot(
            window, temporal_weight[lag_index], preferred_element_type=jnp.float32
        )
    temporal = lax.psum_scatter(
        total.reshape(row_total, frame_count, width_cells, channels).astype(jnp.bfloat16),
        "rows",
        scatter_dimension=0,
        tiled=True,
    ).astype(jnp.float32)
    hidden = (latents.astype(jnp.float32) + temporal + temporal_bias).astype(jnp.bfloat16)
    normed_all = lax.all_gather(layer_norm(hidden, token_gain), "rows", axis=0, tiled=True)
    flat = normed_all.reshape(-1, channels)
    head_cols = query_weight.shape[1]
    head_count = head_cols // HD
    token_count = flat.shape[0]
    queries = jnp.dot(flat, query_weight, preferred_element_type=jnp.float32).astype(jnp.bfloat16)
    keys = jnp.dot(flat, key_weight, preferred_element_type=jnp.float32).astype(jnp.bfloat16)
    values = jnp.dot(flat, value_weight, preferred_element_type=jnp.float32).astype(jnp.bfloat16)
    start_state = (
        jnp.full((token_count, head_count), -1e30, jnp.float32),
        jnp.zeros((token_count, head_count), jnp.float32),
        jnp.zeros((token_count, head_count, HD), jnp.float32),
    )
    local_keys = keys.reshape(token_count, head_count, HD)
    local_values = values.reshape(token_count, head_count, HD)

    def travel(turn, state):
        query_moving, running_max, denominator, numerator = state
        running_max, denominator, numerator = attend(
            query_moving, (running_max, denominator, numerator), local_keys, local_values
        )
        return (
            shifted_2(query_moving, "frames", 1),
            shifted_2(running_max.astype(jnp.bfloat16), "frames", 1).astype(running_max.dtype),
            shifted_2(denominator.astype(jnp.bfloat16), "frames", 1).astype(denominator.dtype),
            shifted_2(numerator.astype(jnp.bfloat16), "frames", 1).astype(numerator.dtype),
        )

    start_moving = queries.reshape(token_count, head_count, HD)
    final = lax.fori_loop(0, lax.axis_size("frames"), travel, (start_moving,) + start_state)
    denominator, numerator = (final[2], final[3])
    attended = (
        (numerator / denominator[..., None])
        .astype(jnp.bfloat16)
        .reshape(plane_rows, frame_count, width_cells, head_cols)
    )
    row_piece = attended
    mixed = lax.psum_scatter(
        jnp.dot(row_piece.reshape(-1, head_cols), output_weight, preferred_element_type=jnp.float32)
        .reshape(row_count * lax.axis_size("rows"), frame_count, width_cells, channels)
        .astype(jnp.bfloat16),
        "rows",
        scatter_dimension=0,
        tiled=True,
    ).astype(jnp.float32)
    return (hidden.astype(jnp.float32) + mixed).astype(jnp.bfloat16)


def solution(mesh):
    in_specs = (
        P("rows", ("groups", "frames"), None, None),
        P(None, None, None, "rows"),
        P("rows"),
        P("rows"),
        P("rows"),
        P(None, "rows", None),
        P(),
        P(),
        P(None, "rows"),
        P(None, "rows"),
        P(None, "rows"),
        P("rows", None),
    )
    out_specs = P("rows", ("groups", "frames"), None, None)
    return jax.shard_map(body, mesh=mesh, in_specs=in_specs, out_specs=out_specs, check_vma=False)
```

profile of v0, /device:TPU:0, one launch (start us, length us, event | category | flops | bytes accessed | tf_op | source)
XLA Modules:
  0.0 143.6 jit_solution(10929822833257368733)
XLA Ops:
  6.5 9.7 %all_gather.6 = bf16[16,1,16,1280]{3,2,1,0:T(8,128)(2,1)S(1)} all-gather(bf16[4,1,16,1280]{3,2,1,0:T(8,128)(2,1)} %param.14), channel_id=1, replica_groups=mesh['groups'=2,'frames'=4,'rows'=4] {'rows'}, dimensions={0}, use_global_device_ids=true | all-gather | bytes 819200 | tf_op jit(solution)/shard_map/all_gather | solution.py:100
  16.2 1.4 %pad_slice_fusion = (bf16[16,1,16,1280]{3,2,1,0:T(8,128)(2,1)S(1)}, bf16[16,1,16,1280]{3,2,1,0:T(8,128)(2,1)S(1)}, bf16[16,1,16,1280]{3,2,1,0:T(8,128)(2,1)S(1)}...) fusion(bf16[16,1,16,1280]{3,2,1,0:T(8,128)(2,1)S(1)} %all_gather.6), kind=kLoop, calls=%fused_computation.20 | loop fusion | bytes 5898240 | tf_op jit(solution)/shard_map/slice | solution.py:37
  17.7 2.1 %fusion.25 = f32[256,320]{0,1:T(8,128)S(1)} fusion(bf16[256,1280]{1,0:T(8,128)(2,1)S(1)} %bitcast.124, bf16[3,3,1280,320]{2,3,1,0:T(8,128)(2,1)} %param.15), kind=kOutput, calls=%fused_computation.52 | convolution fusion | flops 209715200 | bytes 1802240 | tf_op jit(solution)/shard_map/dot_general | solution.py:40
  22.8 0.5 add_reduce_fusion
  24.7 1.4 collective-permute-start.5
  26.1 4.6 %collective-permute-start.4 = (bf16[16,1,16,320]{3,2,0,1:T(8,128)(2,1)S(1)}, bf16[16,1,16,320]{3,2,0,1:T(8,128)(2,1)S(1)}, u32[]{:S(2)}, u32[]{:S(2)}) collective-permute-start(bf16[16,1,16,320]{3,2,0,1:T(8,128)(2,1)S(1)} %multiply_convert_fusion), channel_id=1, source_target_pairs={{0,4},{4,8},{8,12},{1,5},{5,9},{9,13},{2,6},{6,10},{10,14},{3,7},{... | collective-permute-start | bytes 491528 | tf_op jit(solution)/shard_map/ppermute | solution.py:19
  30.7 1.9 %fusion.14 = f32[256,1280]{1,0:T(8,128)S(1)} fusion(bf16[3,320,1280]{2,1,0:T(8,128)(2,1)} %param.19, f32[256,320]{0,1:T(8,128)S(1)} %get-tuple-element.149, f32[320]{0:T(512)S(1)} %copy-done.9, f32[320]{0:T(512)S(1)} %copy-done.10, f32[320]{0:T(512)S(1)} %div.73, f32[320]{0:T(512)S(1)} %sub.56, f32[320]{0:T(512)S(1)} %copy-done.7), kind=kOutput, calls=%fused_computation.41 | convolution fusion | flops 210534400 | bytes 2464000 | tf_op jit(solution)/shard_map/dot_general | solution.py:119
  32.6 1.2 collective-permute-done.5
  34.4 0.7 collective-permute-done.4
  35.1 1.4 fusion.10
  36.5 24.3 %reduce-scatter.3.cloned.1.call-done = bf16[4,1,16,1280]{3,2,0,1:T(8,128)(2,1)} async-done(((bf16[16,1,16,1280]{3,2,0,1:T(8,128)(2,1)}), bf16[4,1,16,1280]{3,2,0,1:T(8,128)(2,1)}) %reduce-scatter.3.cloned.1.call-update) | async-done | bytes 163856 | tf_op jit(solution)/shard_map/reduce_scatter | solution.py:122
  60.8 1.0 convert_reduce_fusion
  62.3 7.5 %all_gather.7 = bf16[16,1,16,1280]{3,2,1,0:T(8,128)(2,1)S(1)} all-gather(bf16[4,1,16,1280]{3,2,1,0:T(8,128)(2,1)S(1)} %fusion.47), channel_id=1, replica_groups=mesh['groups'=2,'frames'=4,'rows'=4] {'rows'}, dimensions={0}, use_global_device_ids=true | all-gather | bytes 819200 | tf_op jit(solution)/shard_map/all_gather | solution.py:129
  70.7 1.5 %convolution_convert_fusion.3 = bf16[256,256]{0,1:T(8,128)(2,1)S(1)} fusion(bf16[256,1280]{1,0:T(8,128)(2,1)S(1)} %bitcast.110, bf16[1280,256]{1,0:T(8,128)(2,1)} %param.22), kind=kOutput, calls=%fused_computation.38 | convolution fusion | flops 167837696 | bytes 1441792 | tf_op jit(solution)/shard_map/dot_general | solution.py:134
  72.2 41.0 %while.16 = (s32[]{:T(128)}, bf16[256,4,64]{0,2,1:T(8,128)(2,1)S(1)}, f32[256,4]{0,1:T(4,128)S(1)}, f32[256,4]{0,1:T(4,128)S(1)}, f32[256,4,64]{0,2,1:T(8,128)S(...) while((s32[]{:T(128)}, ...), condition=%wide.region_10.11_spmd.clone, body=%wide.region_7.10_spmd.clone.sunk | while | flops 69018624 | bytes 5722377 | solution.py:158
  73.1 1.5 %collective-permute-start.3 = (bf16[256,4,64]{0,2,1:T(8,128)(2,1)S(1)}, bf16[256,4,64]{0,2,1:T(8,128)(2,1)S(1)}, u32[]{:S(2)}, u32[]{:S(2)}) collective-permute-start(bf16[256,4,64]{0,2,1:T(8,128)(2,1)S(1)} %fusion.95), channel_id=1, source_target_pairs={{0,4},{4,8},{8,12},{12,0},{1,5},{5,9},{9,13},{13,1},{2,6},{6,10},{... | collective-permute-start | bytes 393224 | tf_op jit(solution)/shard_map/while/body/eval_jaxpr/ppermute | solution.py:28
  74.6 1.5 %collective-permute-start = (bf16[256,4,64]{0,2,1:T(8,128)(2,1)S(1)}, bf16[256,4,64]{0,2,1:T(8,128)(2,1)S(1)}, u32[]{:S(2)}, u32[]{:S(2)}) collective-permute-start(bf16[256,4,64]{0,2,1:T(8,128)(2,1)S(1)} %copy.49), channel_id=1, source_target_pairs={{0,4},{4,8},{8,12},{12,0},{1,5},{5,9},{9,13},{13,1},{2,6},{6,10},{... | collective-permute-start | bytes 393224 | tf_op jit(solution)/shard_map/while/body/eval_jaxpr/ppermute | solution.py:28
  76.1 1.5 %collective-permute-start.2 = (bf16[256,4]{0,1:T(4,128)(2,1)S(1)}, bf16[256,4]{0,1:T(4,128)(2,1)S(1)}, u32[]{:S(2)}, u32[]{:S(2)}) collective-permute-start(bf16[256,4]{0,1:T(4,128)(2,1)S(1)} %get-tuple-element.203), channel_id=1, source_target_pairs={{0,4},{4,8},{8,12},{12,0},{1,5},{5,9},{9,13},{13,1},{2,6},{6,10},{... | collective-permute-start | bytes 6152 | tf_op jit(solution)/shard_map/while/body/eval_jaxpr/ppermute | solution.py:28
  78.1 5.5 %collective-permute-done.2 = bf16[256,4]{0,1:T(4,128)(2,1)S(1)} collective-permute-done((bf16[256,4]{0,1:T(4,128)(2,1)S(1)}, bf16[256,4]{0,1:T(4,128)(2,1)S(1)}, u32[]{:S(2)}, u32[]{:S(2)}) %collective-permute-start.2) | collective-permute-done | bytes 2080 | tf_op jit(solution)/shard_map/while/body/eval_jaxpr/ppermute | solution.py:28
  84.6 1.2 collective-permute-start
  85.7 1.5 %collective-permute-start.2 = (bf16[256,4]{0,1:T(4,128)(2,1)S(1)}, bf16[256,4]{0,1:T(4,128)(2,1)S(1)}, u32[]{:S(2)}, u32[]{:S(2)}) collective-permute-start(bf16[256,4]{0,1:T(4,128)(2,1)S(1)} %get-tuple-element.203), channel_id=1, source_target_pairs={{0,4},{4,8},{8,12},{12,0},{1,5},{5,9},{9,13},{13,1},{2,6},{6,10},{... | collective-permute-start | bytes 6152 | tf_op jit(solution)/shard_map/while/body/eval_jaxpr/ppermute | solution.py:28
  87.2 2.3 %collective-permute-start.1 = (bf16[256,4]{0,1:T(4,128)(2,1)S(1)}, bf16[256,4]{0,1:T(4,128)(2,1)S(1)}, u32[]{:S(2)}, u32[]{:S(2)}) collective-permute-start(bf16[256,4]{0,1:T(4,128)(2,1)S(1)} %get-tuple-element.200), channel_id=1, source_target_pairs={{0,4},{4,8},{8,12},{12,0},{1,5},{5,9},{9,13},{13,1},{2,6},{6,10},{... | collective-permute-start | bytes 6152 | tf_op jit(solution)/shard_map/while/body/eval_jaxpr/ppermute | solution.py:28
  89.5 4.7 %collective-permute-done.2 = bf16[256,4]{0,1:T(4,128)(2,1)S(1)} collective-permute-done((bf16[256,4]{0,1:T(4,128)(2,1)S(1)}, bf16[256,4]{0,1:T(4,128)(2,1)S(1)}, u32[]{:S(2)}, u32[]{:S(2)}) %collective-permute-start.2) | collective-permute-done | bytes 2080 | tf_op jit(solution)/shard_map/while/body/eval_jaxpr/ppermute | solution.py:28
  95.3 0.8 collective-permute-start.2
  96.0 4.1 %collective-permute-start.1 = (bf16[256,4]{0,1:T(4,128)(2,1)S(1)}, bf16[256,4]{0,1:T(4,128)(2,1)S(1)}, u32[]{:S(2)}, u32[]{:S(2)}) collective-permute-start(bf16[256,4]{0,1:T(4,128)(2,1)S(1)} %get-tuple-element.200), channel_id=1, source_target_pairs={{0,4},{4,8},{8,12},{12,0},{1,5},{5,9},{9,13},{13,1},{2,6},{6,10},{... | collective-permute-start | bytes 6152 | tf_op jit(solution)/shard_map/while/body/eval_jaxpr/ppermute | solution.py:28
  100.1 3.7 %collective-permute-done.2 = bf16[256,4]{0,1:T(4,128)(2,1)S(1)} collective-permute-done((bf16[256,4]{0,1:T(4,128)(2,1)S(1)}, bf16[256,4]{0,1:T(4,128)(2,1)S(1)}, u32[]{:S(2)}, u32[]{:S(2)}) %collective-permute-start.2) | collective-permute-done | bytes 2080 | tf_op jit(solution)/shard_map/while/body/eval_jaxpr/ppermute | solution.py:28
  105.0 1.2 collective-permute-start.2
  106.1 3.7 %collective-permute-start.1 = (bf16[256,4]{0,1:T(4,128)(2,1)S(1)}, bf16[256,4]{0,1:T(4,128)(2,1)S(1)}, u32[]{:S(2)}, u32[]{:S(2)}) collective-permute-start(bf16[256,4]{0,1:T(4,128)(2,1)S(1)} %get-tuple-element.200), channel_id=1, source_target_pairs={{0,4},{4,8},{8,12},{12,0},{1,5},{5,9},{9,13},{13,1},{2,6},{6,10},{... | collective-permute-start | bytes 6152 | tf_op jit(solution)/shard_map/while/body/eval_jaxpr/ppermute | solution.py:28
  109.8 3.2 %collective-permute-done.2 = bf16[256,4]{0,1:T(4,128)(2,1)S(1)} collective-permute-done((bf16[256,4]{0,1:T(4,128)(2,1)S(1)}, bf16[256,4]{0,1:T(4,128)(2,1)S(1)}, u32[]{:S(2)}, u32[]{:S(2)}) %collective-permute-start.2) | collective-permute-done | bytes 2080 | tf_op jit(solution)/shard_map/while/body/eval_jaxpr/ppermute | solution.py:28
  113.6 1.2 fusion.11
  114.8 20.3 %reduce-scatter.5.cloned.1.call-done = bf16[4,1,16,1280]{3,2,0,1:T(8,128)(2,1)} async-done(((bf16[16,1,16,1280]{3,2,0,1:T(8,128)(2,1)}), bf16[4,1,16,1280]{3,2,0,1:T(8,128)(2,1)}) %reduce-scatter.5.cloned.1.call-update) | async-done | bytes 163856 | tf_op jit(solution)/shard_map/reduce_scatter | solution.py:166
  135.1 1.6 %fusion.46 = bf16[4,1,16,1280]{3,2,1,0:T(8,128)(2,1)} fusion(bf16[4,1,16,1280]{3,2,0,1:T(8,128)(2,1)} %reduce-scatter.5.cloned.1.call-done, bf16[4,1,16,1280]{3,2,0,1:T(8,128)(2,1)S(1)} %get-tuple-element.137), kind=kLoop, calls=%fused_computation.82 | loop fusion | flops 327680 | bytes 491520 | tf_op jit(solution)/shard_map/convert_element_type | solution.py:174
  (115 shorter events, 10.9 us)
Async XLA Ops:
  6.5 107.1 %copy-start = (bf16[256,1280]{1,0:T(8,128)(2,1)S(1)}, bf16[256,1280]{1,0:T(8,128)(2,1)}, u32[]{:S(2)}) copy-start(bf16[256,1280]{1,0:T(8,128)(2,1)} %param.25) | copy-start | bytes 1966084
  6.5 54.3 %reduce-scatter.3.cloned.1.call-start = ((), (), s32[]{:S(2)}) async-start(), calls=%async_computation.2 | async-start | bytes 819200 | tf_op jit(solution)/shard_map/reduce_scatter | solution.py:122
  16.2 3.6 %copy-start.1 = (bf16[3,3,1280,320]{2,3,1,0:T(8,128)(2,1)S(1)}, bf16[3,3,1280,320]{2,3,1,0:T(8,128)(2,1)}, u32[]{:S(2)}) copy-start(bf16[3,3,1280,320]{2,3,1,0:T(8,128)(2,1)} %param.15) | copy-start | bytes 22118404
  21.9 0.9 copy-start.7
  22.3 2.2 %copy-start.9 = (f32[320]{0:T(512)S(1)}, f32[320]{0:T(512)}, u32[]{:S(2)}) copy-start(f32[320]{0:T(512)} %param.18) | copy-start | bytes 3844
  22.4 2.2 %copy-start.10 = (f32[320]{0:T(512)S(1)}, f32[320]{0:T(512)}, u32[]{:S(2)}) copy-start(f32[320]{0:T(512)} %param.17) | copy-start | bytes 3844
  24.5 9.3 %copy-start.2 = (bf16[3,320,1280]{2,1,0:T(8,128)(2,1)S(1)}, bf16[3,320,1280]{2,1,0:T(8,128)(2,1)}, u32[]{:S(2)}) copy-start(bf16[3,320,1280]{2,1,0:T(8,128)(2,1)} %param.19) | copy-start | bytes 7372804
  24.7 9.2 %collective-permute-start.5 = (bf16[16,1,16,320]{3,2,0,1:T(8,128)(2,1)S(1)}, bf16[16,1,16,320]{3,2,0,1:T(8,128)(2,1)S(1)}, u32[]{:S(2)}, u32[]{:S(2)}) collective-permute-start(bf16[16,1,16,320]{3,2,0,1:T(8,128)(2,1)S(1)} %multiply_convert_fusion), channel_id=1, source_target_pairs={{4,0},{8,4},{12,8},{5,1},{9,5},{13,9},{6,2},{10,6},{14,10},{7,3},{... | collective-permute-start | bytes 491528 | tf_op jit(solution)/shard_map/ppermute | solution.py:20
  26.1 8.9 %collective-permute-start.4 = (bf16[16,1,16,320]{3,2,0,1:T(8,128)(2,1)S(1)}, bf16[16,1,16,320]{3,2,0,1:T(8,128)(2,1)S(1)}, u32[]{:S(2)}, u32[]{:S(2)}) collective-permute-start(bf16[16,1,16,320]{3,2,0,1:T(8,128)(2,1)S(1)} %multiply_convert_fusion), channel_id=1, source_target_pairs={{0,4},{4,8},{8,12},{1,5},{5,9},{9,13},{2,6},{6,10},{10,14},{3,7},{... | collective-permute-start | bytes 491528 | tf_op jit(solution)/shard_map/ppermute | solution.py:19
  35.0 25.8 %copy-start.5 = (bf16[4,1,16,1280]{3,2,1,0:T(8,128)(2,1)S(1)}, bf16[4,1,16,1280]{3,2,1,0:T(8,128)(2,1)}, u32[]{:S(2)}) copy-start(bf16[4,1,16,1280]{3,2,1,0:T(8,128)(2,1)} %param.14) | copy-start | bytes 491524
  35.1 25.8 %copy-start.6 = (f32[1280]{0:T(1024)S(1)}, f32[1280]{0:T(1024)}, u32[]{:S(2)}) copy-start(f32[1280]{0:T(1024)} %param.20) | copy-start | bytes 15364
  35.1 27.1 %copy-start.8 = (f32[1280]{0:T(1024)S(1)}, f32[1280]{0:T(1024)}, u32[]{:S(2)}) copy-start(f32[1280]{0:T(1024)} %param.21) | copy-start | bytes 15364
  35.1 34.7 %copy-start.3 = (bf16[1280,256]{1,0:T(8,128)(2,1)S(1)}, bf16[1280,256]{1,0:T(8,128)(2,1)}, u32[]{:S(2)}) copy-start(bf16[1280,256]{1,0:T(8,128)(2,1)} %param.23) | copy-start | bytes 1966084
  36.4 33.8 %copy-start.4 = (bf16[1280,256]{1,0:T(8,128)(2,1)S(1)}, bf16[1280,256]{1,0:T(8,128)(2,1)}, u32[]{:S(2)}) copy-start(bf16[1280,256]{1,0:T(8,128)(2,1)} %param.24) | copy-start | bytes 1966084
  36.4 98.7 %reduce-scatter.5.cloned.1.call-start = ((), (), s32[]{:S(2)}) async-start(), calls=%async_computation.3 | async-start | bytes 819200 | tf_op jit(solution)/shard_map/reduce_scatter | solution.py:166
  73.1 10.5 %collective-permute-start.3 = (bf16[256,4,64]{0,2,1:T(8,128)(2,1)S(1)}, bf16[256,4,64]{0,2,1:T(8,128)(2,1)S(1)}, u32[]{:S(2)}, u32[]{:S(2)}) collective-permute-start(bf16[256,4,64]{0,2,1:T(8,128)(2,1)S(1)} %fusion.95), channel_id=1, source_target_pairs={{0,4},{4,8},{8,12},{12,0},{1,5},{5,9},{9,13},{13,1},{2,6},{6,10},{... | collective-permute-start | bytes 393224 | tf_op jit(solution)/shard_map/while/body/eval_jaxpr/ppermute | solution.py:28
  74.6 9.0 %collective-permute-start = (bf16[256,4,64]{0,2,1:T(8,128)(2,1)S(1)}, bf16[256,4,64]{0,2,1:T(8,128)(2,1)S(1)}, u32[]{:S(2)}, u32[]{:S(2)}) collective-permute-start(bf16[256,4,64]{0,2,1:T(8,128)(2,1)S(1)} %copy.49), channel_id=1, source_target_pairs={{0,4},{4,8},{8,12},{12,0},{1,5},{5,9},{9,13},{13,1},{2,6},{6,10},{... | collective-permute-start | bytes 393224 | tf_op jit(solution)/shard_map/while/body/eval_jaxpr/ppermute | solution.py:28
  76.1 7.5 %collective-permute-start.2 = (bf16[256,4]{0,1:T(4,128)(2,1)S(1)}, bf16[256,4]{0,1:T(4,128)(2,1)S(1)}, u32[]{:S(2)}, u32[]{:S(2)}) collective-permute-start(bf16[256,4]{0,1:T(4,128)(2,1)S(1)} %get-tuple-element.203), channel_id=1, source_target_pairs={{0,4},{4,8},{8,12},{12,0},{1,5},{5,9},{9,13},{13,1},{2,6},{6,10},{... | collective-permute-start | bytes 6152 | tf_op jit(solution)/shard_map/while/body/eval_jaxpr/ppermute | solution.py:28
  77.6 6.0 %collective-permute-start.1 = (bf16[256,4]{0,1:T(4,128)(2,1)S(1)}, bf16[256,4]{0,1:T(4,128)(2,1)S(1)}, u32[]{:S(2)}, u32[]{:S(2)}) collective-permute-start(bf16[256,4]{0,1:T(4,128)(2,1)S(1)} %get-tuple-element.200), channel_id=1, source_target_pairs={{0,4},{4,8},{8,12},{12,0},{1,5},{5,9},{9,13},{13,1},{2,6},{6,10},{... | collective-permute-start | bytes 6152 | tf_op jit(solution)/shard_map/while/body/eval_jaxpr/ppermute | solution.py:28
  84.5 9.7 %collective-permute-start.3 = (bf16[256,4,64]{0,2,1:T(8,128)(2,1)S(1)}, bf16[256,4,64]{0,2,1:T(8,128)(2,1)S(1)}, u32[]{:S(2)}, u32[]{:S(2)}) collective-permute-start(bf16[256,4,64]{0,2,1:T(8,128)(2,1)S(1)} %fusion.95), channel_id=1, source_target_pairs={{0,4},{4,8},{8,12},{12,0},{1,5},{5,9},{9,13},{13,1},{2,6},{6,10},{... | collective-permute-start | bytes 393224 | tf_op jit(solution)/shard_map/while/body/eval_jaxpr/ppermute | solution.py:28
  84.6 9.7 %collective-permute-start = (bf16[256,4,64]{0,2,1:T(8,128)(2,1)S(1)}, bf16[256,4,64]{0,2,1:T(8,128)(2,1)S(1)}, u32[]{:S(2)}, u32[]{:S(2)}) collective-permute-start(bf16[256,4,64]{0,2,1:T(8,128)(2,1)S(1)} %copy.49), channel_id=1, source_target_pairs={{0,4},{4,8},{8,12},{12,0},{1,5},{5,9},{9,13},{13,1},{2,6},{6,10},{... | collective-permute-start | bytes 393224 | tf_op jit(solution)/shard_map/while/body/eval_jaxpr/ppermute | solution.py:28
  85.7 8.4 %collective-permute-start.2 = (bf16[256,4]{0,1:T(4,128)(2,1)S(1)}, bf16[256,4]{0,1:T(4,128)(2,1)S(1)}, u32[]{:S(2)}, u32[]{:S(2)}) collective-permute-start(bf16[256,4]{0,1:T(4,128)(2,1)S(1)} %get-tuple-element.203), channel_id=1, source_target_pairs={{0,4},{4,8},{8,12},{12,0},{1,5},{5,9},{9,13},{13,1},{2,6},{6,10},{... | collective-permute-start | bytes 6152 | tf_op jit(solution)/shard_map/while/body/eval_jaxpr/ppermute | solution.py:28
  87.2 7.0 %collective-permute-start.1 = (bf16[256,4]{0,1:T(4,128)(2,1)S(1)}, bf16[256,4]{0,1:T(4,128)(2,1)S(1)}, u32[]{:S(2)}, u32[]{:S(2)}) collective-permute-start(bf16[256,4]{0,1:T(4,128)(2,1)S(1)} %get-tuple-element.200), channel_id=1, source_target_pairs={{0,4},{4,8},{8,12},{12,0},{1,5},{5,9},{9,13},{13,1},{2,6},{6,10},{... | collective-permute-start | bytes 6152 | tf_op jit(solution)/shard_map/while/body/eval_jaxpr/ppermute | solution.py:28
  95.1 8.8 %collective-permute-start.3 = (bf16[256,4,64]{0,2,1:T(8,128)(2,1)S(1)}, bf16[256,4,64]{0,2,1:T(8,128)(2,1)S(1)}, u32[]{:S(2)}, u32[]{:S(2)}) collective-permute-start(bf16[256,4,64]{0,2,1:T(8,128)(2,1)S(1)} %fusion.95), channel_id=1, source_target_pairs={{0,4},{4,8},{8,12},{12,0},{1,5},{5,9},{9,13},{13,1},{2,6},{6,10},{... | collective-permute-start | bytes 393224 | tf_op jit(solution)/shard_map/while/body/eval_jaxpr/ppermute | solution.py:28
  95.2 8.7 %collective-permute-start = (bf16[256,4,64]{0,2,1:T(8,128)(2,1)S(1)}, bf16[256,4,64]{0,2,1:T(8,128)(2,1)S(1)}, u32[]{:S(2)}, u32[]{:S(2)}) collective-permute-start(bf16[256,4,64]{0,2,1:T(8,128)(2,1)S(1)} %copy.49), channel_id=1, source_target_pairs={{0,4},{4,8},{8,12},{12,0},{1,5},{5,9},{9,13},{13,1},{2,6},{6,10},{... | collective-permute-start | bytes 393224 | tf_op jit(solution)/shard_map/while/body/eval_jaxpr/ppermute | solution.py:28
  95.3 8.6 %collective-permute-start.2 = (bf16[256,4]{0,1:T(4,128)(2,1)S(1)}, bf16[256,4]{0,1:T(4,128)(2,1)S(1)}, u32[]{:S(2)}, u32[]{:S(2)}) collective-permute-start(bf16[256,4]{0,1:T(4,128)(2,1)S(1)} %get-tuple-element.203), channel_id=1, source_target_pairs={{0,4},{4,8},{8,12},{12,0},{1,5},{5,9},{9,13},{13,1},{2,6},{6,10},{... | collective-permute-start | bytes 6152 | tf_op jit(solution)/shard_map/while/body/eval_jaxpr/ppermute | solution.py:28
  96.0 7.8 %collective-permute-start.1 = (bf16[256,4]{0,1:T(4,128)(2,1)S(1)}, bf16[256,4]{0,1:T(4,128)(2,1)S(1)}, u32[]{:S(2)}, u32[]{:S(2)}) collective-permute-start(bf16[256,4]{0,1:T(4,128)(2,1)S(1)} %get-tuple-element.200), channel_id=1, source_target_pairs={{0,4},{4,8},{8,12},{12,0},{1,5},{5,9},{9,13},{13,1},{2,6},{6,10},{... | collective-permute-start | bytes 6152 | tf_op jit(solution)/shard_map/while/body/eval_jaxpr/ppermute | solution.py:28
  104.8 8.3 %collective-permute-start.3 = (bf16[256,4,64]{0,2,1:T(8,128)(2,1)S(1)}, bf16[256,4,64]{0,2,1:T(8,128)(2,1)S(1)}, u32[]{:S(2)}, u32[]{:S(2)}) collective-permute-start(bf16[256,4,64]{0,2,1:T(8,128)(2,1)S(1)} %fusion.95), channel_id=1, source_target_pairs={{0,4},{4,8},{8,12},{12,0},{1,5},{5,9},{9,13},{13,1},{2,6},{6,10},{... | collective-permute-start | bytes 393224 | tf_op jit(solution)/shard_map/while/body/eval_jaxpr/ppermute | solution.py:28
  104.9 8.2 %collective-permute-start = (bf16[256,4,64]{0,2,1:T(8,128)(2,1)S(1)}, bf16[256,4,64]{0,2,1:T(8,128)(2,1)S(1)}, u32[]{:S(2)}, u32[]{:S(2)}) collective-permute-start(bf16[256,4,64]{0,2,1:T(8,128)(2,1)S(1)} %copy.49), channel_id=1, source_target_pairs={{0,4},{4,8},{8,12},{12,0},{1,5},{5,9},{9,13},{13,1},{2,6},{6,10},{... | collective-permute-start | bytes 393224 | tf_op jit(solution)/shard_map/while/body/eval_jaxpr/ppermute | solution.py:28
  105.0 8.1 %collective-permute-start.2 = (bf16[256,4]{0,1:T(4,128)(2,1)S(1)}, bf16[256,4]{0,1:T(4,128)(2,1)S(1)}, u32[]{:S(2)}, u32[]{:S(2)}) collective-permute-start(bf16[256,4]{0,1:T(4,128)(2,1)S(1)} %get-tuple-element.203), channel_id=1, source_target_pairs={{0,4},{4,8},{8,12},{12,0},{1,5},{5,9},{9,13},{13,1},{2,6},{6,10},{... | collective-permute-start | bytes 6152 | tf_op jit(solution)/shard_map/while/body/eval_jaxpr/ppermute | solution.py:28
  106.1 7.0 %collective-permute-start.1 = (bf16[256,4]{0,1:T(4,128)(2,1)S(1)}, bf16[256,4]{0,1:T(4,128)(2,1)S(1)}, u32[]{:S(2)}, u32[]{:S(2)}) collective-permute-start(bf16[256,4]{0,1:T(4,128)(2,1)S(1)} %get-tuple-element.200), channel_id=1, source_target_pairs={{0,4},{4,8},{8,12},{12,0},{1,5},{5,9},{9,13},{13,1},{2,6},{6,10},{... | collective-permute-start | bytes 6152 | tf_op jit(solution)/shard_map/while/body/eval_jaxpr/ppermute | solution.py:28
Sparse Core Ops, SparseCore 0:
  36.6 24.2 reduce-scatter.2
  114.9 20.1 reduce-scatter.4
where the time goes:
time: 144 us
  waiting for transfers between devices  63.8 us (44%)
  starting transfers between devices  26 us (18%)
  blocking collectives  17.2 us (12%)
  matrix products  15.4 us (11%)
  between operations  13.7 us (10%)
  other arithmetic  4.55 us (3%)
  local copies, waits for them, and re-layouts  2.76 us (2%)
    reduce_scatter x1, waiting for transfers between devices, body(): lax.psum_scatter(total.reshape(row_total, frame_count, width_cells, chann...  24.3 us
    reduce_scatter x1, waiting for transfers between devices, body(): lax.psum_scatter(jnp.dot(row_piece.reshape(-1, head_cols), output_weight,...  20.3 us
    ppermute x16, starting transfers between devices, shifted_2(): return lax.ppermute(value, axis, pairs)  20 us
    ppermute x16, waiting for transfers between devices, shifted_2(): return lax.ppermute(value, axis, pairs)  17.2 us
    all_gather x1, blocking collectives, body(): plane = lax.all_gather(latents, 'rows', axis=0, tiled=True)  9.66 us
    all_gather x1, blocking collectives, body(): lax.all_gather(layer_norm(hidden, token_gain), 'rows', axis=0, tiled=True)  7.5 us
    dot_general x9, matrix products, conv_plane(): jnp.dot(window, weight[row_off, col_off], preferred_element_type=jnp.floa...  5.56 us
    ppermute x1, starting transfers between devices, padded_2(): before = lax.ppermute(last, axis, up)  4.56 us
  transfers between devices with their start and end apart: 20, of which 8 were waited for; matrix products, arithmetic and copies ran while one was open for 2% of the time, Pallas kernels for 0%

commit v1 on v0

v1 whole, which is shorter than its diff:
```python
import functools
import math

import jax
import jax.numpy as jnp
from jax import lax
from jax.experimental import pallas as pl
from jax.experimental.pallas import tpu as pltpu
from jax.sharding import PartitionSpec as P

HD = 64
NORM_GROUPS = 32
VMEM_LIMIT = 16 * 1024 * 1024


def swap(array, axis, stride):
    size = lax.axis_size(axis)
    return lax.ppermute(array, axis, [(i, i ^ stride) for i in range(size)])


def neighbours(array, axis):
    size = lax.axis_size(axis)
    even = [(i, i ^ 1) for i in range(size) if i ^ 1 < size]
    odd = [(i, ((i + 1) ^ 1) - 1) for i in range(1, size) if ((i + 1) ^ 1) - 1 < size]
    return lax.ppermute(array, axis, even), lax.ppermute(array, axis, odd)


def load_kernel(*refs):
    half = len(refs) // 2
    sems = refs[-1]
    copies = [
        pltpu.make_async_copy(source, target, sems.at[i])
        for i, (source, target) in enumerate(zip(refs[:half], refs[half : 2 * half]))
    ]
    for copy in copies:
        copy.start()
    for copy in copies:
        copy.wait()


def load(*arrays):
    return pl.pallas_call(
        load_kernel,
        out_shape=[jax.ShapeDtypeStruct(a.shape, a.dtype) for a in arrays],
        in_specs=[pl.BlockSpec(memory_space=pltpu.HBM)] * len(arrays),
        out_specs=[pl.BlockSpec(memory_space=pltpu.VMEM)] * len(arrays),
        scratch_shapes=[pltpu.SemaphoreType.DMA((len(arrays),))],
        compiler_params=pltpu.CompilerParams(vmem_limit_bytes=VMEM_LIMIT),
        cost_estimate=pl.CostEstimate(
            flops=0, bytes_accessed=sum(a.size * a.dtype.itemsize for a in arrays), transcendentals=0
        ),
    )(*arrays)


def conv_kernel(*refs, pieces, cols, groups, axis):
    plane_refs = refs[:pieces]
    weight_ref, bias_ref, gain_ref, shift_ref, out_ref, padded_ref = refs[pieces:]
    share, chans = plane_refs[0].shape
    tokens = pieces * share
    outs = out_ref.shape[0]
    padded_ref[0:cols] = jnp.zeros((cols, chans), padded_ref.dtype)
    padded_ref[cols + tokens : tokens + 2 * cols] = jnp.zeros((cols, chans), padded_ref.dtype)
    index = lax.axis_index(axis)
    for mask, piece in enumerate(plane_refs):
        start = pl.multiple_of((index ^ mask) * share + cols, math.gcd(share, cols))
        padded_ref[pl.ds(start, share)] = piece[...]
    total = None
    for row_off in range(3):
        window = padded_ref[row_off * cols : row_off * cols + tokens]
        weight = weight_ref[row_off].reshape(3 * outs, chans)
        term = lax.dot_general(
            weight, window, (((1,), (1,)), ((), ())), preferred_element_type=jnp.float32
        )
        total = term if total is None else total + term
    column = lax.broadcasted_iota(jnp.int32, (outs, tokens), 1) % cols
    left = jnp.where(column == 0, 0.0, pltpu.roll(total[:outs], 1, 1))
    right = jnp.where(column == cols - 1, 0.0, pltpu.roll(total[2 * outs :], tokens - 1, 1))

    diagonal = lax.broadcasted_iota(jnp.int32, (outs, outs), 0) == lax.broadcasted_iota(
        jnp.int32, (outs, outs), 1
    )

    def upright(row):
        return jnp.sum(jnp.where(diagonal, row[None], 0.0), axis=1, keepdims=True)

    spatial = total[outs : 2 * outs] + left + right + upright(bias_ref[...])
    per_group = outs // groups
    count = per_group * tokens

    def group_mean(values):
        sums = jnp.sum(values, axis=1, keepdims=True).reshape(groups, per_group, 1)
        sums = jnp.sum(sums, axis=1, keepdims=True) * (1.0 / count)
        return jnp.broadcast_to(sums, (groups, per_group, 1)).reshape(outs, 1)

    centred = spatial - group_mean(spatial)
    inverse = 1.0 / jnp.sqrt(group_mean(centred * centred) + 1e-05)
    scaled = centred * (inverse * upright(gain_ref[...])) + upright(shift_ref[...])
    out_ref[...] = (scaled / (1.0 + jnp.exp(-scaled))).astype(out_ref.dtype)


def conv_norm(pieces, weight, bias, gain, shift, cols, groups, rows_axis):
    share, chans = pieces[0].shape
    tokens, outs = share * len(pieces), weight.shape[2]
    return pl.pallas_call(
        functools.partial(
            conv_kernel, pieces=len(pieces), cols=cols, groups=groups, axis=rows_axis
        ),
        out_shape=jax.ShapeDtypeStruct((outs, tokens), jnp.bfloat16),
        in_specs=[pl.BlockSpec(memory_space=pltpu.VMEM)] * (len(pieces) + 4),
        out_specs=pl.BlockSpec(memory_space=pltpu.VMEM),
        scratch_shapes=[pltpu.VMEM((tokens + 2 * cols, chans), jnp.bfloat16)],
        compiler_params=pltpu.CompilerParams(vmem_limit_bytes=VMEM_LIMIT),
        cost_estimate=pl.CostEstimate(
            flops=18 * tokens * outs * chans,
            bytes_accessed=2 * (weight.size + tokens * chans + outs * tokens),
            transcendentals=outs * tokens,
        ),
    )(*pieces, weight, bias, gain, shift)


def spread_kernel(*refs, places, frames_axis, rows_axis):
    pieces = refs[: len(places)]
    weight_ref, send_ref, keep_ref, stack_ref, total_ref = refs[len(places) :]
    k = pieces[0].shape[0]
    inner_count, outer_count, width, _ = total_ref.shape
    is_odd = lax.rem(lax.axis_index(frames_axis), 2)
    for piece, (even, odd) in zip(pieces, places):
        start = even * k if even == odd else pl.multiple_of((even + is_odd * (odd - even)) * k, 16)
        stack_ref[pl.ds(start, k)] = piece[...]
    total = lax.dot_general(
        stack_ref[...],
        weight_ref[...],
        (((0,), (0,)), ((), ())),
        preferred_element_type=jnp.float32,
    )
    for outer in range(outer_count):
        for inner in range(inner_count):
            start = (outer * inner_count + inner) * width
            total_ref[inner, outer] = total[start : start + width]
    mine = lax.rem(lax.axis_index(rows_axis), inner_count)
    send_ref[...] = total_ref[1 - mine].astype(send_ref.dtype)
    keep_ref[...] = total_ref[mine]


def spread(pieces, places, weight, outer_count, frames_axis, rows_axis):
    k, tokens = pieces[0].shape
    channels = weight.shape[1]
    part = (outer_count, tokens // (2 * outer_count), channels)
    return pl.pallas_call(
        functools.partial(
            spread_kernel, places=places, frames_axis=frames_axis, rows_axis=rows_axis
        ),
        out_shape=[
            jax.ShapeDtypeStruct(part, jnp.bfloat16),
            jax.ShapeDtypeStruct(part, jnp.float32),
        ],
        in_specs=[pl.BlockSpec(memory_space=pltpu.VMEM)] * (len(pieces) + 1),
        out_specs=[pl.BlockSpec(memory_space=pltpu.VMEM)] * 2,
        scratch_shapes=[
            pltpu.VMEM((len(pieces) * k, tokens), jnp.bfloat16),
            pltpu.VMEM((2,) + part, jnp.float32),
        ],
        compiler_params=pltpu.CompilerParams(vmem_limit_bytes=VMEM_LIMIT),
        cost_estimate=pl.CostEstimate(
            flops=2 * len(pieces) * tokens * k * channels,
            bytes_accessed=2 * weight.size + 6 * tokens * channels,
            transcendentals=0,
        ),
    )(*pieces, weight)


def merge_kernel(mine_ref, theirs_ref, *refs, axis, inner_count):
    place = lax.div(lax.axis_index(axis), inner_count)
    for mask, (send_ref, keep_ref) in enumerate(zip(refs[::2], refs[1::2])):
        total = mine_ref[place ^ mask] + theirs_ref[place ^ mask].astype(jnp.float32)
        send_ref[...] = total.astype(send_ref.dtype)
        keep_ref[...] = total


def merge(mine, theirs, rows_axis, inner_count):
    shapes = [
        jax.ShapeDtypeStruct(theirs.shape[1:], dtype) for dtype in (jnp.bfloat16, jnp.float32)
    ] * theirs.shape[0]
    outs = pl.pallas_call(
        functools.partial(merge_kernel, axis=rows_axis, inner_count=inner_count),
        out_shape=shapes,
        in_specs=[pl.BlockSpec(memory_space=pltpu.VMEM)] * 2,
        out_specs=[pl.BlockSpec(memory_space=pltpu.VMEM)] * len(shapes),
        compiler_params=pltpu.CompilerParams(vmem_limit_bytes=VMEM_LIMIT),
        cost_estimate=pl.CostEstimate(
            flops=theirs.size, bytes_accessed=12 * theirs.size, transcendentals=0
        ),
    )(mine, theirs)
    return outs[::2], outs[1::2]


def deal_kernel(own_ref, pair_ref, out_ref, *, frames_axis, rows_axis, inner_count):
    _, rows, width, _ = out_ref.shape
    is_odd = lax.rem(lax.axis_index(frames_axis), 2)
    index = lax.axis_index(rows_axis)
    for source, frame in ((own_ref, is_odd), (pair_ref, 1 - is_odd)):
        for mask in range(rows):
            place = mask // inner_count * inner_count + lax.rem(index ^ mask, inner_count)
            start = pl.multiple_of(place * width, width)
            out_ref[frame, index ^ mask] = source[pl.ds(start, width)]


def deal(own, pair, rows, frames_axis, rows_axis, inner_count):
    tokens, columns = own.shape
    return pl.pallas_call(
        functools.partial(
            deal_kernel, frames_axis=frames_axis, rows_axis=rows_axis, inner_count=inner_count
        ),
        out_shape=jax.ShapeDtypeStruct((2, rows, tokens // rows, columns), jnp.bfloat16),
        in_specs=[pl.BlockSpec(memory_space=pltpu.VMEM)] * 2,
        out_specs=pl.BlockSpec(memory_space=pltpu.VMEM),
        compiler_params=pltpu.CompilerParams(vmem_limit_bytes=VMEM_LIMIT),
        cost_estimate=pl.CostEstimate(
            flops=0, bytes_accessed=8 * tokens * columns, transcendentals=0
        ),
    )(own, pair)


def finish_kernel(attended_ref, *refs, axis):
    weights, (hidden_ref, out_ref) = refs[:-2], refs[-2:]
    index = lax.axis_index(axis)
    total = hidden_ref[...].astype(jnp.float32)
    for mask, weight in enumerate(weights):
        halves = [attended_ref[frame, index ^ mask] for frame in range(2)]
        columns = jnp.concatenate(halves, axis=1)
        total = total + jnp.dot(columns, weight[...], preferred_element_type=jnp.float32)
    out_ref[...] = total.astype(out_ref.dtype)


def finish(attended, weights, hidden, rows_axis):
    return pl.pallas_call(
        functools.partial(finish_kernel, axis=rows_axis),
        out_shape=jax.ShapeDtypeStruct(hidden.shape, hidden.dtype),
        in_specs=[pl.BlockSpec(memory_space=pltpu.VMEM)] * (len(weights) + 2),
        out_specs=pl.BlockSpec(memory_space=pltpu.VMEM),
        compiler_params=pltpu.CompilerParams(vmem_limit_bytes=VMEM_LIMIT),
        cost_estimate=pl.CostEstimate(
            flops=2 * hidden.shape[0] * len(weights) * weights[0].size,
            bytes_accessed=2 * len(weights) * weights[0].size + 4 * hidden.size,
            transcendentals=0,
        ),
    )(attended, *weights, hidden)


def norm_kernel(latents_ref, mine_ref, theirs_ref, bias_ref, gain_ref, normed_ref, *hidden_refs):
    temporal = mine_ref[...] + theirs_ref[...].astype(jnp.float32) + bias_ref[...][None]
    hidden = latents_ref[...].astype(jnp.float32) + temporal
    hidden = hidden.astype(normed_ref.dtype)
    for hidden_ref in hidden_refs:
        hidden_ref[...] = hidden
    flat = hidden.astype(jnp.float32)
    scale = 1.0 / flat.shape[-1]
    shifted = flat - jnp.sum(flat, axis=-1, keepdims=True) * scale
    variance = jnp.sum(shifted * shifted, axis=-1, keepdims=True) * scale
    normed = shifted * (1.0 / jnp.sqrt(variance + 1e-05)) * gain_ref[...][None]
    normed_ref[...] = normed.astype(normed_ref.dtype)


def norm_of_hidden(latents, mine, theirs, bias, gain, with_hidden):
    shapes = [jax.ShapeDtypeStruct(theirs.shape, jnp.bfloat16)] * (2 if with_hidden else 1)
    return pl.pallas_call(
        norm_kernel,
        out_shape=shapes,
        in_specs=[pl.BlockSpec(memory_space=pltpu.VMEM)] * 5,
        out_specs=[pl.BlockSpec(memory_space=pltpu.VMEM)] * len(shapes),
        compiler_params=pltpu.CompilerParams(vmem_limit_bytes=VMEM_LIMIT),
        cost_estimate=pl.CostEstimate(
            flops=12 * theirs.size, bytes_accessed=12 * theirs.size, transcendentals=0
        ),
    )(latents, mine, theirs, bias, gain)


def project_kernel(*refs, pieces, frames_axis, rows_axis):
    q_ref, k_ref, v_ref, own_q, own_kv, pair_qkv, pair_kv, flat_ref, scratch = refs[pieces:]
    index = lax.axis_index(rows_axis)
    for mask, piece in enumerate(refs[:pieces]):
        flat_ref[lax.rem(index ^ mask, pieces)] = piece[...]
    flat = flat_ref[...].reshape(-1, flat_ref.shape[-1])
    _, _, share, _, tokens = scratch.shape
    for which, weight_ref in enumerate((q_ref, k_ref, v_ref)):
        product = jnp.dot(flat, weight_ref[...], preferred_element_type=jnp.float32)
        upright = product.T.astype(scratch.dtype)
        scratch[:, which] = upright.reshape(2, share, HD, tokens)
    is_odd = lax.rem(lax.axis_index(frames_axis), 2)
    own_q[...] = scratch[is_odd, 0]
    own_kv[...] = scratch[is_odd, 1:]
    pair_qkv[...] = scratch[1 - is_odd]
    pair_kv[...] = scratch[1 - is_odd, 1:]


def project(pieces, query_weight, key_weight, value_weight, frames_axis, rows_axis):
    width, channels = pieces[0].shape
    tokens = len(pieces) * width
    share = query_weight.shape[1] // HD // 2

    def shape(count):
        return jax.ShapeDtypeStruct((count, share, HD, tokens), jnp.bfloat16)

    return pl.pallas_call(
        functools.partial(
            project_kernel, pieces=len(pieces), frames_axis=frames_axis, rows_axis=rows_axis
        ),
        out_shape=[
            jax.ShapeDtypeStruct((share, HD, tokens), jnp.bfloat16),
            shape(2),
            shape(3),
            shape(2),
        ],
        in_specs=[pl.BlockSpec(memory_space=pltpu.VMEM)] * (len(pieces) + 3),
        out_specs=[pl.BlockSpec(memory_space=pltpu.VMEM)] * 4,
        scratch_shapes=[
            pltpu.VMEM((len(pieces), width, channels), jnp.bfloat16),
            pltpu.VMEM((2, 3, share, HD, tokens), jnp.bfloat16),
        ],
        compiler_params=pltpu.CompilerParams(vmem_limit_bytes=VMEM_LIMIT),
        cost_estimate=pl.CostEstimate(
            flops=6 * tokens * channels * query_weight.shape[1],
            bytes_accessed=6 * query_weight.size + 2 * tokens * channels,
            transcendentals=0,
        ),
    )(*pieces, query_weight, key_weight, value_weight)


def attention_kernel(*refs, parts, kv_count, first, last):
    own_q, kvs = refs[:parts], refs[parts : parts + kv_count]
    rest = refs[parts + kv_count :]
    pair_qkv, rest = rest[:parts], rest[parts:]
    state, outs = ((), rest) if first else (rest[:3], rest[3:])
    scale = 1.0 / math.sqrt(HD)
    contract_first = (((0,), (0,)), ((), ()))

    def wide(arrays):
        return jnp.concatenate(list(arrays), axis=1)

    for head in range(own_q[0].shape[0]):
        pairs = [(kv[0, head], kv[1, head]) for kv in kvs]
        if first:
            pairs += [(qkv[1, head], qkv[2, head]) for qkv in pair_qkv]
        groups = [pairs[i : i + parts] for i in range(0, len(pairs), parts)]
        keys = [wide(key for key, _ in group) for group in groups]
        values = [wide(value for _, value in group) for group in groups]
        asked = (wide(q[head] for q in own_q), wide(qkv[0, head] for qkv in pair_qkv))
        for which, query in enumerate(asked):
            query = (query.astype(jnp.float32) * scale).astype(jnp.bfloat16)
            scores = [
                lax.dot_general(key, query, contract_first, preferred_element_type=jnp.float32)
                for key in keys
            ]
            peak = functools.reduce(
                jnp.maximum, [jnp.max(s, axis=0, keepdims=True) for s in scores]
            )
            if first:
                denominator = jnp.zeros_like(peak)
                numerator = jnp.zeros((HD, query.shape[1]), jnp.float32)
            else:
                old_peak, denominator, numerator = (ref[head, which] for ref in state)
                peak = jnp.maximum(peak, old_peak)
                shrink = jnp.exp(old_peak - peak)
                denominator, numerator = denominator * shrink, numerator * shrink
            for value, score in zip(values, scores):
                weights = jnp.exp(score - peak)
                denominator = denominator + jnp.sum(weights, axis=0, keepdims=True)
                numerator = numerator + jnp.dot(
                    value, weights.astype(jnp.bfloat16), preferred_element_type=jnp.float32
                )
            if last:
                out = outs[which]
                result = (numerator / denominator).T
                out[:, head * HD : (head + 1) * HD] = result.astype(out.dtype)
            else:
                for ref, value in zip(outs, (peak, denominator, numerator)):
                    ref[head, which] = value


def attend(own_q, pair_qkv, kvs, state, last):
    parts = len(own_q)
    heads, _, width = own_q[0].shape
    tokens = parts * width
    keys = (len(kvs) + (0 if state else parts)) * width
    if last:
        shapes = [jax.ShapeDtypeStruct((tokens, heads * HD), jnp.bfloat16)] * 2
    else:
        shapes = [
            jax.ShapeDtypeStruct((heads, 2, rows, tokens), jnp.float32) for rows in (1, 1, HD)
        ]
    work = 2 * heads * tokens * keys
    args = (*own_q, *kvs, *pair_qkv, *state)
    return pl.pallas_call(
        functools.partial(
            attention_kernel, parts=parts, kv_count=len(kvs), first=not state, last=last
        ),
        out_shape=shapes,
        in_specs=[pl.BlockSpec(memory_space=pltpu.VMEM)] * len(args),
        out_specs=[pl.BlockSpec(memory_space=pltpu.VMEM)] * len(shapes),
        compiler_params=pltpu.CompilerParams(vmem_limit_bytes=VMEM_LIMIT),
        cost_estimate=pl.CostEstimate(
            flops=4 * work * HD,
            bytes_accessed=sum(a.size * a.dtype.itemsize for a in args),
            transcendentals=work,
        ),
    )(*args)


def body(
    latents,
    spatial_weight,
    spatial_bias,
    norm_gain,
    norm_shift,
    temporal_weight,
    temporal_bias,
    token_gain,
    query_weight,
    key_weight,
    value_weight,
    output_weight,
):
    rows_size, frames_size = lax.axis_size("rows"), lax.axis_size("frames")
    row_count, frame_count, width_cells, channels = latents.shape
    if rows_size != 4 or frames_size < 2 or frames_size & (frames_size - 1) or frame_count != 1:
        raise NotImplementedError("mesh shape")
    inner_size = 2
    outer_size = rows_size // inner_size
    loaded = load(jnp.swapaxes(spatial_weight, 2, 3))
    own = latents.reshape(-1, channels)
    pieces = {0: own}
    bit = rows_size // 2
    while bit > 1:
        pieces.update({m | bit: swap(piece, "rows", bit) for m, piece in pieces.items()})
        bit //= 2
    far, loaded, output_weight = lax.optimization_barrier(
        ({m: pieces[m] for m in pieces if m}, loaded, output_weight)
    )
    pieces.update(far)
    weights = {m: swap(output_weight, "rows", m) for m in (inner_size, 1)}
    weights[0] = output_weight
    pieces.update({m | 1: swap(piece, "rows", 1) for m, piece in pieces.items()})
    pieces = [pieces[m] for m in range(rows_size)]
    local_out = spatial_weight.shape[3]
    activated = conv_norm(
        pieces,
        *loaded,
        spatial_bias,
        norm_gain,
        norm_shift,
        width_cells,
        NORM_GROUPS // rows_size,
        "rows",
    )
    first, second = neighbours(activated, "frames")
    send, chip_sum = spread(
        [activated, first, second],
        ((1, 1), (2, 0), (0, 2)),
        temporal_weight.reshape(3 * local_out, channels),
        outer_size,
        "frames",
        "rows",
    )
    sends, keeps = merge(chip_sum, swap(send, "rows", 1), "rows", inner_size)
    sends, weights = lax.optimization_barrier((sends, weights))
    weights[inner_size + 1] = swap(weights[inner_size], "rows", 1)
    others = [swap(sends[1 - mask], "rows", inner_size) for mask in range(outer_size)]
    own_q, own_kv, pair_qkv, far = [], [], [], []
    for mask in range(outer_size):
        latent_rows, other = pieces[mask * inner_size], others[mask]
        if mask:
            other, weights = lax.optimization_barrier((other, weights))
        normed, *wanted = norm_of_hidden(
            latent_rows, keeps[mask], other, temporal_bias, token_gain, mask == 0
        )
        hidden = wanted[0] if wanted else hidden
        q, kv, *sent = project(
            [normed, swap(normed, "rows", 1)],
            query_weight,
            key_weight,
            value_weight,
            "frames",
            "rows",
        )
        own_q.append(q)
        own_kv.append(kv)
        far.append(
            [
                swap(sent[1] if m % 2 else kv, "frames", m)
                for m in range(frames_size - 1, 1, -1)
            ]
        )
        pair_qkv.append(swap(sent[0], "frames", 1))
    early, late = own_kv + far[0][:1], far[0][1:] + far[1]
    state = attend(own_q, pair_qkv, early, (), not late)
    own_out, pair_out = attend(own_q, pair_qkv, late, state, True) if late else state
    dealt = deal(own_out, pair_out, rows_size, "frames", "rows", inner_size)
    together = 2 * rows_size
    groups = [
        list(range(start, start + together))
        for start in range(0, frames_size * rows_size, together)
    ]
    arrived = lax.all_to_all(
        dealt.reshape((together,) + dealt.shape[2:]),
        ("frames", "rows"),
        0,
        0,
        axis_index_groups=groups,
        tiled=True,
    )
    weights = [weights[m] for m in range(rows_size)]
    result = finish(arrived.reshape(dealt.shape), weights, hidden, "rows")
    return result.reshape(latents.shape)


def solution(mesh):
    in_specs = (
        P("rows", ("groups", "frames"), None, None),
        P(None, None, None, "rows"),
        P("rows"),
        P("rows"),
        P("rows"),
        P(None, "rows", None),
        P(),
        P(),
        P(None, "rows"),
        P(None, "rows"),
        P(None, "rows"),
        P("rows", None),
    )
    out_specs = P("rows", ("groups", "frames"), None, None)
    return jax.shard_map(body, mesh=mesh, in_specs=in_specs, out_specs=out_specs, check_vma=False)
```

time: 144 us -> 64.5 us (0.45)
  waiting for transfers between devices: 63.8 us -> 21.4 us
  matrix products: 15.4 us -> 0 us
  between operations: 13.7 us -> 0.24 us
  Pallas kernels: 0 us -> 10.5 us
  blocking collectives: 17.2 us -> 7.75 us
  starting transfers between devices: 26 us -> 21.2 us
  other arithmetic: 4.55 us -> 0 us
    reduce_scatter x2 -> x0, waiting for transfers between devices: 44.6 us -> none  [the longest x1 24.3 us: body(): lax.psum_scatter(total.reshape(row_total, frame_count, width_cells, chann...]
    all_gather x2 -> x0, blocking collectives: 17.2 us -> none  [the longest x1 9.66 us: body(): plane = lax.all_gather(latents, 'rows', axis=0, tiled=True)]
    dot_general x24 -> x0, matrix products: 15.4 us -> none  [the longest x9 5.56 us: conv_plane(): jnp.dot(window, weight[row_off, col_off], preferred_element_type=jnp.floa...]
    pallas_call x0 -> x12, Pallas kernels: none -> 10.5 us  [the longest x2 3.24 us: attend(): pl.pallas_call(functools.partial(attention_kernel, parts=parts, kv_count=...]
    all_to_all x0 -> x1, blocking collectives: none -> 7.75 us  [body(): lax.all_to_all(dealt.reshape((together,) + dealt.shape[2:]), ('frames', '...]
    ppermute x18 -> x19, starting transfers between devices: 25.9 us -> 21.2 us  [the longest x17 16.1 us: swap(): return lax.ppermute(array, axis, [(i, i ^ stride) for i in range(size)])]
    unnamed x24, local copies, waits for them, and re-layouts: 0.26 us -> 3.15 us
    reduce_sum x9 -> x0, other arithmetic: 2.39 us -> none  [the longest x1 1.04 us: layer_norm(): token_mean = jnp.mean(flat, axis=-1, keepdims=True)]
  transfers between devices with their start and end apart: 20 -> 19, of which waited for: 8 -> 9; matrix products, arithmetic and copies ran while one was open for 2% -> 0% of each run, Pallas kernels for 0% -> 12%
where the time goes in v1:
time: 64.5 us; the launch traced here: 64.4 us
  waiting for transfers between devices  21.4 us (33%)
  starting transfers between devices  21.2 us (33%)
  Pallas kernels  10.5 us (16%)
  blocking collectives  7.75 us (12%)
  local copies, waits for them, and re-layouts  3.15 us (5%)
    ppermute x17, waiting for transfers between devices, swap(): return lax.ppermute(array, axis, [(i, i ^ stride) for i in range(size)])  17.1 us
    ppermute x17, starting transfers between devices, swap(): return lax.ppermute(array, axis, [(i, i ^ stride) for i in range(size)])  16.1 us
    all_to_all x1, blocking collectives, body(): lax.all_to_all(dealt.reshape((together,) + dealt.shape[2:]), ('frames', '...  7.75 us
    ppermute x2, starting transfers between devices, neighbours(): return (lax.ppermute(array, axis, even), lax.ppermute(array, axis, odd))  5.13 us
    ppermute x2, waiting for transfers between devices, neighbours(): return (lax.ppermute(array, axis, even), lax.ppermute(array, axis, odd))  4.37 us
    pallas_call x2, Pallas kernels, attend(): pl.pallas_call(functools.partial(attention_kernel, parts=parts, kv_count=...  3.24 us
    unnamed x24, local copies, waits for them, and re-layouts  3.15 us
    pallas_call x1, Pallas kernels, conv_norm(): pl.pallas_call(functools.partial(conv_kernel, pieces=len(pieces), cols=co...  2.56 us
  transfers between devices with their start and end apart: 19, of which 9 were waited for; matrix products, arithmetic and copies ran while one was open for 0% of the time, Pallas kernels for 12%

profile of v1, /device:TPU:0, one launch (start us, length us, event | category | flops | bytes accessed | tf_op | source)
XLA Modules:
  0.0 64.4 jit_solution(6938584296667851369)
XLA Ops:
  0.0 2.9 %collective-permute-start.1 = (bf16[64,1280]{1,0:T(8,128)(2,1)}, bf16[64,1280]{1,0:T(8,128)(2,1)S(1)}, u32[]{:S(2)}, u32[]{:S(2)}) collective-permute-start(bf16[64,1280]{1,0:T(8,128)(2,1)} %bitcast.10), channel_id=1, source_target_pairs={{0,2},{1,3},{2,0},{3,1},{4,6},{5,7},{6,4},{7,5},{8,10},{9,11},{10,... | collective-permute-start | bytes 491528 | tf_op jit(solution)/shard_map/ppermute | solution.py:18
  2.9 3.1 %copy-done = bf16[3,3,1280,320]{2,3,1,0:T(8,128)(2,1)S(1)} copy-done((bf16[3,3,1280,320]{2,3,1,0:T(8,128)(2,1)S(1)}, bf16[3,3,1280,320]{2,3,1,0:T(8,128)(2,1)}, u32[]{:S(2)}) %copy-start) | copy-done | bytes 7372824
  6.1 0.6 shard_map.118.refs_4_
  6.7 0.7 %collective-permute-done.1.refs_2_.latents_ref = bf16[64,1280]{1,0:T(8,128)(2,1)S(1)} collective-permute-done((bf16[64,1280]{1,0:T(8,128)(2,1)}, bf16[64,1280]{1,0:T(8,128)(2,1)S(1)}, u32[]{:S(2)}, u32[]{:S(2)}) %collective-permute-start.1) | collective-permute-done | bytes 163872 | tf_op jit(solution)/shard_map/ppermute | solution.py:18
  7.4 1.7 %collective-permute-start.7 = (bf16[256,1280]{1,0:T(8,128)(2,1)S(1)}, bf16[256,1280]{1,0:T(8,128)(2,1)S(1)}, u32[]{:S(2)}, u32[]{:S(2)}) collective-permute-start(bf16[256,1280]{1,0:T(8,128)(2,1)S(1)} %copy-done.5), channel_id=1, source_target_pairs={{0,2},{1,3},{2,0},{3,1},{4,6},{5,7},{6,4},{7,5},{8,10},{9,11},{10,... | collective-permute-start | bytes 1966088 | tf_op jit(solution)/shard_map/ppermute | solution.py:18
  9.1 0.2 collective-permute-start.6
  9.4 2.6 %shard_map.119.refs_0_ = bf16[320,256]{1,0:T(8,128)(2,1)S(1)} custom-call(bf16[64,1280]{1,0:T(8,128)(2,1)S(1)} %bitcast.12, bf16[64,1280]{1,0:T(8,128)(2,1)S(1)} %collective-permute-done.refs_1_, bf16[64,1280]{1,0:T(8,128)(2,1)S(1)} %collective-permute-done.1.refs_2_.latents_ref, bf16[64,1280]{1,0:T(8,128)(2,1)S(1)} %collective-permute-done.2.refs_3_, ...), custom_call_target="tpu_custom_call" | custom-call | flops 1887436800 | bytes 8192000 | tf_op jit(solution)/shard_map/pallas_call | solution.py:104
  11.9 0.7 %collective-permute-start.4 = (bf16[320,256]{1,0:T(8,128)(2,1)S(1)}, bf16[320,256]{1,0:T(8,128)(2,1)S(1)}, u32[]{:S(2)}, u32[]{:S(2)}) collective-permute-start(bf16[320,256]{1,0:T(8,128)(2,1)S(1)} %shard_map.119.refs_0_), channel_id=1, source_target_pairs={{4,8},{8,4},{5,9},{9,5},{6,10},{10,6},{7,11},{11,7},{20,24},{24,20... | collective-permute-start | bytes 491528 | tf_op jit(solution)/shard_map/ppermute | solution.py:25
  12.6 4.5 %collective-permute-start.3 = (bf16[320,256]{1,0:T(8,128)(2,1)S(1)}, bf16[320,256]{1,0:T(8,128)(2,1)S(1)}, u32[]{:S(2)}, u32[]{:S(2)}) collective-permute-start(bf16[320,256]{1,0:T(8,128)(2,1)S(1)} %shard_map.119.refs_0_), channel_id=1, source_target_pairs={{0,4},{4,0},{8,12},{12,8},{1,5},{5,1},{9,13},{13,9},{2,6},{6,2},{1... | collective-permute-start | bytes 491528 | tf_op jit(solution)/shard_map/ppermute | solution.py:25
  17.1 4.4 %collective-permute-done.3.refs_1_ = bf16[320,256]{1,0:T(8,128)(2,1)S(1)} collective-permute-done((bf16[320,256]{1,0:T(8,128)(2,1)S(1)}, bf16[320,256]{1,0:T(8,128)(2,1)S(1)}, u32[]{:S(2)}, u32[]{:S(2)}) %collective-permute-start.3) | collective-permute-done | bytes 163872 | tf_op jit(solution)/shard_map/ppermute | solution.py:25
  21.4 1.1 %shard_map.120 = (bf16[2,64,1280]{2,1,0:T(8,128)(2,1)S(1)}, f32[2,64,1280]{2,1,0:T(8,128)S(1)}) custom-call(bf16[320,256]{1,0:T(8,128)(2,1)S(1)} %shard_map.119.refs_0_, bf16[320,256]{1,0:T(8,128)(2,1)S(1)} %collective-permute-done.3.refs_1_, bf16[320,256]{1,0:T(8,128)(2,1)S(1)} %collective-permute-done.4.refs_2_, bf16[960,1280]{1,0:T(8,128)(2,1)S(1)} %bitcast.9), custom_call_target="tpu_custom_call" | custom-call | flops 629145600 | bytes 4423680 | tf_op jit(solution)/shard_map/pallas_call | solution.py:149
  22.6 1.6 %collective-permute-done.5.theirs_ref = bf16[2,64,1280]{2,1,0:T(8,128)(2,1)S(1)} collective-permute-done((bf16[2,64,1280]{2,1,0:T(8,128)(2,1)S(1)}, bf16[2,64,1280]{2,1,0:T(8,128)(2,1)S(1)}, u32[]{:S(2)}, u32[]{:S(2)}) %collective-permute-start.5) | collective-permute-done | bytes 327712 | tf_op jit(solution)/shard_map/ppermute | solution.py:18
  24.3 0.2 collective-permute-done.7.refs_2_
  24.5 1.7 %collective-permute-start.8 = (bf16[64,1280]{1,0:T(8,128)(2,1)S(1)}, bf16[64,1280]{1,0:T(8,128)(2,1)S(1)}, u32[]{:S(2)}, u32[]{:S(2)}) collective-permute-start(bf16[64,1280]{1,0:T(8,128)(2,1)S(1)} %get-tuple-element.47), channel_id=1, source_target_pairs={{0,2},{1,3},{2,0},{3,1},{4,6},{5,7},{6,4},{7,5},{8,10},{9,11},{10,... | collective-permute-start | bytes 491528 | tf_op jit(solution)/shard_map/ppermute | solution.py:18
  26.2 0.3 collective-permute-start.10
  26.5 5.0 %collective-permute-done.8.theirs_ref = bf16[64,1280]{1,0:T(8,128)(2,1)S(1)} collective-permute-done((bf16[64,1280]{1,0:T(8,128)(2,1)S(1)}, bf16[64,1280]{1,0:T(8,128)(2,1)S(1)}, u32[]{:S(2)}, u32[]{:S(2)}) %collective-permute-start.8) | collective-permute-done | bytes 163872 | tf_op jit(solution)/shard_map/ppermute | solution.py:18
  31.5 0.3 shard_map.122
  31.9 2.7 %collective-permute-done.10.theirs_ref = bf16[64,1280]{1,0:T(8,128)(2,1)S(1)} collective-permute-done((bf16[64,1280]{1,0:T(8,128)(2,1)S(1)}, bf16[64,1280]{1,0:T(8,128)(2,1)S(1)}, u32[]{:S(2)}, u32[]{:S(2)}) %collective-permute-start.10) | collective-permute-done | bytes 163872 | tf_op jit(solution)/shard_map/ppermute | solution.py:18
  34.6 0.3 shard_map.124.refs_0_
  35.0 0.6 shard_map.123
  35.6 3.9 %collective-permute-start.18 = (bf16[2,2,64,128]{3,2,1,0:T(8,128)(2,1)S(1)}, bf16[2,2,64,128]{3,2,1,0:T(8,128)(2,1)S(1)}, u32[]{:S(2)}, u32[]{:S(2)}) collective-permute-start(bf16[2,2,64,128]{3,2,1,0:T(8,128)(2,1)S(1)} %get-tuple-element.62), channel_id=1, source_target_pairs={{0,12},{4,8},{8,4},{12,0},{1,13},{5,9},{9,5},{13,1},{2,14},{6,10},... | collective-permute-start | bytes 196616 | tf_op jit(solution)/shard_map/ppermute | solution.py:18
  39.6 0.6 shard_map.125
  40.2 2.1 %collective-permute-start.17 = (bf16[3,2,64,128]{3,2,1,0:T(8,128)(2,1)S(1)}, bf16[3,2,64,128]{3,2,1,0:T(8,128)(2,1)S(1)}, u32[]{:S(2)}, u32[]{:S(2)}) collective-permute-start(bf16[3,2,64,128]{3,2,1,0:T(8,128)(2,1)S(1)} %get-tuple-element.61), channel_id=1, source_target_pairs={{0,4},{4,0},{8,12},{12,8},{1,5},{5,1},{9,13},{13,9},{2,6},{6,2},{1... | collective-permute-start | bytes 294920 | tf_op jit(solution)/shard_map/ppermute | solution.py:18
  42.3 2.4 %collective-permute-start.14 = (bf16[2,2,64,128]{3,2,1,0:T(8,128)(2,1)S(1)}, bf16[2,2,64,128]{3,2,1,0:T(8,128)(2,1)S(1)}, u32[]{:S(2)}, u32[]{:S(2)}) collective-permute-start(bf16[2,2,64,128]{3,2,1,0:T(8,128)(2,1)S(1)} %get-tuple-element.58), channel_id=1, source_target_pairs={{0,12},{4,8},{8,4},{12,0},{1,13},{5,9},{9,5},{13,1},{2,14},{6,10},... | collective-permute-start | bytes 196616 | tf_op jit(solution)/shard_map/ppermute | solution.py:18
  44.7 0.5 collective-permute-start.15
  45.2 2.2 %collective-permute-done.17.refs_6_ = bf16[3,2,64,128]{3,2,1,0:T(8,128)(2,1)S(1)} collective-permute-done((bf16[3,2,64,128]{3,2,1,0:T(8,128)(2,1)S(1)}, bf16[3,2,64,128]{3,2,1,0:T(8,128)(2,1)S(1)}, u32[]{:S(2)}, u32[]{:S(2)}) %collective-permute-start.17) | collective-permute-done | bytes 98336 | tf_op jit(solution)/shard_map/ppermute | solution.py:18
  47.4 1.8 %shard_map.126 = (f32[2,2,1,256]{3,2,1,0:T(1,128)S(1)}, f32[2,2,1,256]{3,2,1,0:T(1,128)S(1)}, f32[2,2,64,256]{3,2,1,0:T(8,128)S(1)}) custom-call(bf16[2,64,128]{2,1,0:T(8,128)(2,1)S(1)} %get-tuple-element.49.refs_0_, bf16[2,64,128]{2,1,0:T(8,128)(2,1)S(1)} %get-tuple-element.56.refs_1_, bf16[2,2,64,128]{3,2,1,0:T(8,128)(2,1)S(1)} %get-tuple-element.57.refs_2_, ...), custom_call_target="tpu_custom_call" | custom-call | flops 167772160 | bytes 458752 | tf_op jit(solution)/shard_map/pallas_call | solution.py:393
  49.2 3.0 %collective-permute-done.13.refs_2_ = bf16[2,2,64,128]{3,2,1,0:T(8,128)(2,1)S(1)} collective-permute-done((bf16[2,2,64,128]{3,2,1,0:T(8,128)(2,1)S(1)}, bf16[2,2,64,128]{3,2,1,0:T(8,128)(2,1)S(1)}, u32[]{:S(2)}, u32[]{:S(2)}) %collective-permute-start.13) | collective-permute-done | bytes 65568 | tf_op jit(solution)/shard_map/ppermute | solution.py:18
  52.2 1.6 %collective-permute-done.15.refs_4_ = bf16[2,2,64,128]{3,2,1,0:T(8,128)(2,1)S(1)} collective-permute-done((bf16[2,2,64,128]{3,2,1,0:T(8,128)(2,1)S(1)}, bf16[2,2,64,128]{3,2,1,0:T(8,128)(2,1)S(1)}, u32[]{:S(2)}, u32[]{:S(2)}) %collective-permute-start.15) | collective-permute-done | bytes 65568 | tf_op jit(solution)/shard_map/ppermute | solution.py:18
  53.8 1.5 %shard_map.127 = (bf16[256,128]{1,0:T(8,128)(2,1)S(1)}, bf16[256,128]{1,0:T(8,128)(2,1)S(1)}) custom-call(bf16[2,64,128]{2,1,0:T(8,128)(2,1)S(1)} %get-tuple-element.49.refs_0_, bf16[2,64,128]{2,1,0:T(8,128)(2,1)S(1)} %get-tuple-element.56.refs_1_, bf16[2,2,64,128]{3,2,1,0:T(8,128)(2,1)S(1)} %collective-permute-done.13.refs_2_, ...), custom_call_target="tpu_custom_call" | custom-call | flops 100663296 | bytes 729088 | tf_op jit(solution)/shard_map/pallas_call | solution.py:393
  55.4 7.7 %all_to_all.5 = bf16[8,64,128]{2,1,0:T(8,128)(2,1)S(1)} all-to-all(bf16[8,64,128]{2,1,0:T(8,128)(2,1)S(1)} %bitcast.15), channel_id=1, replica_groups={{0,1,2,3,4,5,6,7},{8,9,10,11,12,13,14,15},{16,17,18,19,20,21,22,23},{24..., dimensions={0} | all-to-all | bytes 262144 | tf_op jit(solution)/shard_map/all_to_all | solution.py:503
  63.1 1.2 %shard_map.129 = bf16[64,1280]{1,0:T(8,128)(2,1)} custom-call(bf16[2,4,64,128]{3,2,1,0:T(8,128)(2,1)S(1)} %bitcast.14, bf16[256,1280]{1,0:T(8,128)(2,1)S(1)} %copy-done.5, bf16[256,1280]{1,0:T(8,128)(2,1)S(1)} %collective-permute-done.6.refs_1_, bf16[256,1280]{1,0:T(8,128)(2,1)S(1)} %collective-permute-done.7.refs_2_, ...), custom_call_target="tpu_custom_call" | custom-call | flops 167772160 | bytes 2949120 | tf_op jit(solution)/shard_map/pallas_call | solution.py:236
  (43 shorter events, 0.4 us)
Async XLA Ops:
  0.0 7.3 %collective-permute-start.1 = (bf16[64,1280]{1,0:T(8,128)(2,1)}, bf16[64,1280]{1,0:T(8,128)(2,1)S(1)}, u32[]{:S(2)}, u32[]{:S(2)}) collective-permute-start(bf16[64,1280]{1,0:T(8,128)(2,1)} %bitcast.10), channel_id=1, source_target_pairs={{0,2},{1,3},{2,0},{3,1},{4,6},{5,7},{6,4},{7,5},{8,10},{9,11},{10,... | collective-permute-start | bytes 491528 | tf_op jit(solution)/shard_map/ppermute | solution.py:18
  2.9 6.4 %collective-permute-start = (bf16[64,1280]{1,0:T(8,128)(2,1)}, bf16[64,1280]{1,0:T(8,128)(2,1)S(1)}, u32[]{:S(2)}, u32[]{:S(2)}) collective-permute-start(bf16[64,1280]{1,0:T(8,128)(2,1)} %bitcast.11), channel_id=1, source_target_pairs={{0,1},{1,0},{2,3},{3,2},{4,5},{5,4},{6,7},{7,6},{8,9},{9,8},{10,11... | collective-permute-start | bytes 491528 | tf_op jit(solution)/shard_map/ppermute | solution.py:18
  2.9 3.1 %copy-start = (bf16[3,3,1280,320]{2,3,1,0:T(8,128)(2,1)S(1)}, bf16[3,3,1280,320]{2,3,1,0:T(8,128)(2,1)}, u32[]{:S(2)}) copy-start(bf16[3,3,1280,320]{2,3,1,0:T(8,128)(2,1)} %param.13) | copy-start | bytes 22118404
  6.0 1.3 %copy-start.5 = (bf16[256,1280]{1,0:T(8,128)(2,1)S(1)}, bf16[256,1280]{1,0:T(8,128)(2,1)}, u32[]{:S(2)}) copy-start(bf16[256,1280]{1,0:T(8,128)(2,1)} %refs_0_) | copy-start | bytes 1966084
  6.0 3.3 %copy-start.6 = (bf16[4,1,16,1280]{3,2,1,0:T(8,128)(2,1)S(1)}, bf16[4,1,16,1280]{3,2,1,0:T(8,128)(2,1)}, u32[]{:S(2)}) copy-start(bf16[4,1,16,1280]{3,2,1,0:T(8,128)(2,1)} %param.12) | copy-start | bytes 491524
  6.0 3.3 %copy-start.9 = (f32[320]{0:T(512)S(1)}, f32[320]{0:T(512)}, u32[]{:S(2)}) copy-start(f32[320]{0:T(512)} %refs_5_.1) | copy-start | bytes 3844
  6.0 3.3 %copy-start.10 = (f32[320]{0:T(512)S(1)}, f32[320]{0:T(512)}, u32[]{:S(2)}) copy-start(f32[320]{0:T(512)} %refs_6_.1) | copy-start | bytes 3844
  6.0 3.3 %copy-start.11 = (f32[320]{0:T(512)S(1)}, f32[320]{0:T(512)}, u32[]{:S(2)}) copy-start(f32[320]{0:T(512)} %refs_7_.1) | copy-start | bytes 3844
  6.6 14.8 %copy-start.4 = (bf16[3,320,1280]{2,1,0:T(8,128)(2,1)S(1)}, bf16[3,320,1280]{2,1,0:T(8,128)(2,1)}, u32[]{:S(2)}) copy-start(bf16[3,320,1280]{2,1,0:T(8,128)(2,1)} %param.17) | copy-start | bytes 7372804
  6.6 24.9 %copy-start.7 = (f32[1280]{0:T(1024)S(1)}, f32[1280]{0:T(1024)}, u32[]{:S(2)}) copy-start(f32[1280]{0:T(1024)} %bias_ref.3) | copy-start | bytes 15364
  6.6 24.9 %copy-start.8 = (f32[1280]{0:T(1024)S(1)}, f32[1280]{0:T(1024)}, u32[]{:S(2)}) copy-start(f32[1280]{0:T(1024)} %gain_ref.3) | copy-start | bytes 15364
  6.7 28.4 %copy-start.1 = (bf16[1280,256]{1,0:T(8,128)(2,1)S(1)}, bf16[1280,256]{1,0:T(8,128)(2,1)}, u32[]{:S(2)}) copy-start(bf16[1280,256]{1,0:T(8,128)(2,1)} %refs_2_.3) | copy-start | bytes 1966084
  6.7 28.3 %copy-start.2 = (bf16[1280,256]{1,0:T(8,128)(2,1)S(1)}, bf16[1280,256]{1,0:T(8,128)(2,1)}, u32[]{:S(2)}) copy-start(bf16[1280,256]{1,0:T(8,128)(2,1)} %refs_3_.3) | copy-start | bytes 1966084
  6.7 28.3 %copy-start.3 = (bf16[1280,256]{1,0:T(8,128)(2,1)S(1)}, bf16[1280,256]{1,0:T(8,128)(2,1)}, u32[]{:S(2)}) copy-start(bf16[1280,256]{1,0:T(8,128)(2,1)} %refs_4_.3) | copy-start | bytes 1966084
  7.3 2.0 %collective-permute-start.2 = (bf16[64,1280]{1,0:T(8,128)(2,1)S(1)}, bf16[64,1280]{1,0:T(8,128)(2,1)S(1)}, u32[]{:S(2)}, u32[]{:S(2)}) collective-permute-start(bf16[64,1280]{1,0:T(8,128)(2,1)S(1)} %collective-permute-done.1.refs_2_.latents_ref), channel_id=1, source_target_pairs={{0,1},{1,0},{2,3},{3,2},{4,5},{5,4},{6,7},{7,6},{8,9},{9,8},{10,11... | collective-permute-start | bytes 491528 | tf_op jit(solution)/shard_map/ppermute | solution.py:18
  7.4 17.1 %collective-permute-start.7 = (bf16[256,1280]{1,0:T(8,128)(2,1)S(1)}, bf16[256,1280]{1,0:T(8,128)(2,1)S(1)}, u32[]{:S(2)}, u32[]{:S(2)}) collective-permute-start(bf16[256,1280]{1,0:T(8,128)(2,1)S(1)} %copy-done.5), channel_id=1, source_target_pairs={{0,2},{1,3},{2,0},{3,1},{4,6},{5,7},{6,4},{7,5},{8,10},{9,11},{10,... | collective-permute-start | bytes 1966088 | tf_op jit(solution)/shard_map/ppermute | solution.py:18
  9.1 15.4 %collective-permute-start.6 = (bf16[256,1280]{1,0:T(8,128)(2,1)S(1)}, bf16[256,1280]{1,0:T(8,128)(2,1)S(1)}, u32[]{:S(2)}, u32[]{:S(2)}) collective-permute-start(bf16[256,1280]{1,0:T(8,128)(2,1)S(1)} %copy-done.5), channel_id=1, source_target_pairs={{0,1},{1,0},{2,3},{3,2},{4,5},{5,4},{6,7},{7,6},{8,9},{9,8},{10,11... | collective-permute-start | bytes 1966088 | tf_op jit(solution)/shard_map/ppermute | solution.py:18
  11.9 5.1 %collective-permute-start.4 = (bf16[320,256]{1,0:T(8,128)(2,1)S(1)}, bf16[320,256]{1,0:T(8,128)(2,1)S(1)}, u32[]{:S(2)}, u32[]{:S(2)}) collective-permute-start(bf16[320,256]{1,0:T(8,128)(2,1)S(1)} %shard_map.119.refs_0_), channel_id=1, source_target_pairs={{4,8},{8,4},{5,9},{9,5},{6,10},{10,6},{7,11},{11,7},{20,24},{24,20... | collective-permute-start | bytes 491528 | tf_op jit(solution)/shard_map/ppermute | solution.py:25
  12.6 8.8 %collective-permute-start.3 = (bf16[320,256]{1,0:T(8,128)(2,1)S(1)}, bf16[320,256]{1,0:T(8,128)(2,1)S(1)}, u32[]{:S(2)}, u32[]{:S(2)}) collective-permute-start(bf16[320,256]{1,0:T(8,128)(2,1)S(1)} %shard_map.119.refs_0_), channel_id=1, source_target_pairs={{0,4},{4,0},{8,12},{12,8},{1,5},{5,1},{9,13},{13,9},{2,6},{6,2},{1... | collective-permute-start | bytes 491528 | tf_op jit(solution)/shard_map/ppermute | solution.py:25
  22.5 1.7 %collective-permute-start.5 = (bf16[2,64,1280]{2,1,0:T(8,128)(2,1)S(1)}, bf16[2,64,1280]{2,1,0:T(8,128)(2,1)S(1)}, u32[]{:S(2)}, u32[]{:S(2)}) collective-permute-start(bf16[2,64,1280]{2,1,0:T(8,128)(2,1)S(1)} %get-tuple-element.42), channel_id=1, source_target_pairs={{0,1},{1,0},{2,3},{3,2},{4,5},{5,4},{6,7},{7,6},{8,9},{9,8},{10,11... | collective-permute-start | bytes 983048 | tf_op jit(solution)/shard_map/ppermute | solution.py:18
  24.5 10.1 %collective-permute-start.11 = (bf16[256,1280]{1,0:T(8,128)(2,1)S(1)}, bf16[256,1280]{1,0:T(8,128)(2,1)S(1)}, u32[]{:S(2)}, u32[]{:S(2)}) collective-permute-start(bf16[256,1280]{1,0:T(8,128)(2,1)S(1)} %collective-permute-done.7.refs_2_), channel_id=1, source_target_pairs={{0,1},{1,0},{2,3},{3,2},{4,5},{5,4},{6,7},{7,6},{8,9},{9,8},{10,11... | collective-permute-start | bytes 1966088 | tf_op jit(solution)/shard_map/ppermute | solution.py:18
  24.5 7.0 %collective-permute-start.8 = (bf16[64,1280]{1,0:T(8,128)(2,1)S(1)}, bf16[64,1280]{1,0:T(8,128)(2,1)S(1)}, u32[]{:S(2)}, u32[]{:S(2)}) collective-permute-start(bf16[64,1280]{1,0:T(8,128)(2,1)S(1)} %get-tuple-element.47), channel_id=1, source_target_pairs={{0,2},{1,3},{2,0},{3,1},{4,6},{5,7},{6,4},{7,5},{8,10},{9,11},{10,... | collective-permute-start | bytes 491528 | tf_op jit(solution)/shard_map/ppermute | solution.py:18
  26.2 8.4 %collective-permute-start.10 = (bf16[64,1280]{1,0:T(8,128)(2,1)S(1)}, bf16[64,1280]{1,0:T(8,128)(2,1)S(1)}, u32[]{:S(2)}, u32[]{:S(2)}) collective-permute-start(bf16[64,1280]{1,0:T(8,128)(2,1)S(1)} %get-tuple-element.51), channel_id=1, source_target_pairs={{0,2},{1,3},{2,0},{3,1},{4,6},{5,7},{6,4},{7,5},{8,10},{9,11},{10,... | collective-permute-start | bytes 491528 | tf_op jit(solution)/shard_map/ppermute | solution.py:18
  31.8 3.2 %collective-permute-start.9 = (bf16[64,1280]{1,0:T(8,128)(2,1)S(1)}, bf16[64,1280]{1,0:T(8,128)(2,1)S(1)}, u32[]{:S(2)}, u32[]{:S(2)}) collective-permute-start(bf16[64,1280]{1,0:T(8,128)(2,1)S(1)} %get-tuple-element.48.refs_0_), channel_id=1, source_target_pairs={{0,1},{1,0},{2,3},{3,2},{4,5},{5,4},{6,7},{7,6},{8,9},{9,8},{10,11... | collective-permute-start | bytes 491528 | tf_op jit(solution)/shard_map/ppermute | solution.py:18
  34.9 4.7 %collective-permute-start.12 = (bf16[64,1280]{1,0:T(8,128)(2,1)S(1)}, bf16[64,1280]{1,0:T(8,128)(2,1)S(1)}, u32[]{:S(2)}, u32[]{:S(2)}) collective-permute-start(bf16[64,1280]{1,0:T(8,128)(2,1)S(1)} %shard_map.124.refs_0_), channel_id=1, source_target_pairs={{0,1},{1,0},{2,3},{3,2},{4,5},{5,4},{6,7},{7,6},{8,9},{9,8},{10,11... | collective-permute-start | bytes 491528 | tf_op jit(solution)/shard_map/ppermute | solution.py:18
  35.6 9.1 %collective-permute-start.18 = (bf16[2,2,64,128]{3,2,1,0:T(8,128)(2,1)S(1)}, bf16[2,2,64,128]{3,2,1,0:T(8,128)(2,1)S(1)}, u32[]{:S(2)}, u32[]{:S(2)}) collective-permute-start(bf16[2,2,64,128]{3,2,1,0:T(8,128)(2,1)S(1)} %get-tuple-element.62), channel_id=1, source_target_pairs={{0,12},{4,8},{8,4},{12,0},{1,13},{5,9},{9,5},{13,1},{2,14},{6,10},... | collective-permute-start | bytes 196616 | tf_op jit(solution)/shard_map/ppermute | solution.py:18
  39.6 5.6 %collective-permute-start.16 = (bf16[3,2,64,128]{3,2,1,0:T(8,128)(2,1)S(1)}, bf16[3,2,64,128]{3,2,1,0:T(8,128)(2,1)S(1)}, u32[]{:S(2)}, u32[]{:S(2)}) collective-permute-start(bf16[3,2,64,128]{3,2,1,0:T(8,128)(2,1)S(1)} %get-tuple-element.60), channel_id=1, source_target_pairs={{0,4},{4,0},{8,12},{12,8},{1,5},{5,1},{9,13},{13,9},{2,6},{6,2},{1... | collective-permute-start | bytes 294920 | tf_op jit(solution)/shard_map/ppermute | solution.py:18
  40.2 7.2 %collective-permute-start.17 = (bf16[3,2,64,128]{3,2,1,0:T(8,128)(2,1)S(1)}, bf16[3,2,64,128]{3,2,1,0:T(8,128)(2,1)S(1)}, u32[]{:S(2)}, u32[]{:S(2)}) collective-permute-start(bf16[3,2,64,128]{3,2,1,0:T(8,128)(2,1)S(1)} %get-tuple-element.61), channel_id=1, source_target_pairs={{0,4},{4,0},{8,12},{12,8},{1,5},{5,1},{9,13},{13,9},{2,6},{6,2},{1... | collective-permute-start | bytes 294920 | tf_op jit(solution)/shard_map/ppermute | solution.py:18
  42.3 9.9 %collective-permute-start.13 = (bf16[2,2,64,128]{3,2,1,0:T(8,128)(2,1)S(1)}, bf16[2,2,64,128]{3,2,1,0:T(8,128)(2,1)S(1)}, u32[]{:S(2)}, u32[]{:S(2)}) collective-permute-start(bf16[2,2,64,128]{3,2,1,0:T(8,128)(2,1)S(1)} %get-tuple-element.57.refs_2_), channel_id=1, source_target_pairs={{0,8},{4,12},{8,0},{12,4},{1,9},{5,13},{9,1},{13,5},{2,10},{6,14},... | collective-permute-start | bytes 196616 | tf_op jit(solution)/shard_map/ppermute | solution.py:18
  42.3 9.9 %collective-permute-start.14 = (bf16[2,2,64,128]{3,2,1,0:T(8,128)(2,1)S(1)}, bf16[2,2,64,128]{3,2,1,0:T(8,128)(2,1)S(1)}, u32[]{:S(2)}, u32[]{:S(2)}) collective-permute-start(bf16[2,2,64,128]{3,2,1,0:T(8,128)(2,1)S(1)} %get-tuple-element.58), channel_id=1, source_target_pairs={{0,12},{4,8},{8,4},{12,0},{1,13},{5,9},{9,5},{13,1},{2,14},{6,10},... | collective-permute-start | bytes 196616 | tf_op jit(solution)/shard_map/ppermute | solution.py:18
  44.7 9.1 %collective-permute-start.15 = (bf16[2,2,64,128]{3,2,1,0:T(8,128)(2,1)S(1)}, bf16[2,2,64,128]{3,2,1,0:T(8,128)(2,1)S(1)}, u32[]{:S(2)}, u32[]{:S(2)}) collective-permute-start(bf16[2,2,64,128]{3,2,1,0:T(8,128)(2,1)S(1)} %get-tuple-element.59.refs_3_), channel_id=1, source_target_pairs={{0,8},{4,12},{8,0},{12,4},{1,9},{5,13},{9,1},{13,5},{2,10},{6,14},... | collective-permute-start | bytes 196616 | tf_op jit(solution)/shard_map/ppermute | solution.py:18

commit v2 on v1

--- a/solution.py
+++ b/solution.py
@@ -118,55 +118,69 @@
     )(*pieces, weight, bias, gain, shift)
 
 
-def spread_kernel(*refs, places, frames_axis, rows_axis):
+def spread_kernel(*refs, places, parity_axes, rows_axis):
     pieces = refs[: len(places)]
-    weight_ref, send_ref, keep_ref, stack_ref, total_ref = refs[len(places) :]
+    weight_ref, send_ref, rest_ref, stack_ref, rows_ref = refs[len(places) :]
     k = pieces[0].shape[0]
-    inner_count, outer_count, width, _ = total_ref.shape
-    is_odd = lax.rem(lax.axis_index(frames_axis), 2)
+    outer_count, width, _ = rest_ref.shape
+    inner_count = rows_ref.shape[0] // outer_count
+    is_odd = lax.rem(sum(lax.axis_index(axis) for axis in parity_axes), 2)
     for piece, (even, odd) in zip(pieces, places):
         start = even * k if even == odd else pl.multiple_of((even + is_odd * (odd - even)) * k, 16)
         stack_ref[pl.ds(start, k)] = piece[...]
-    total = lax.dot_general(
-        stack_ref[...],
-        weight_ref[...],
-        (((0,), (0,)), ((), ())),
-        preferred_element_type=jnp.float32,
-    )
+    rows_ref[...] = stack_ref[...].T.reshape(rows_ref.shape)
+    mine = lax.rem(lax.axis_index(rows_axis), inner_count)
+    sent = [rows_ref[outer * inner_count + 1 - mine] for outer in range(outer_count)]
+    product = jnp.dot(
+        jnp.concatenate(sent, axis=0), weight_ref[...], preferred_element_type=jnp.float32
+    )
+    send_ref[...] = product.astype(send_ref.dtype).reshape(send_ref.shape)
     for outer in range(outer_count):
-        for inner in range(inner_count):
-            start = (outer * inner_count + inner) * width
-            total_ref[inner, outer] = total[start : start + width]
-    mine = lax.rem(lax.axis_index(rows_axis), inner_count)
-    send_ref[...] = total_ref[1 - mine].astype(send_ref.dtype)
-    keep_ref[...] = total_ref[mine]
-
-
-def spread(pieces, places, weight, outer_count, frames_axis, rows_axis):
+        rest_ref[outer] = rows_ref[outer * inner_count + mine]
+
+
+def keep_kernel(rest_ref, weight_ref, keep_ref):
+    rest = rest_ref[...].reshape(-1, rest_ref.shape[-1])
+    product = jnp.dot(rest, weight_ref[...], preferred_element_type=jnp.float32)
+    keep_ref[...] = product.reshape(keep_ref.shape)
+
+
+def spread(pieces, places, weight, outer_count, parity_axes, rows_axis):
     k, tokens = pieces[0].shape
-    channels = weight.shape[1]
-    part = (outer_count, tokens // (2 * outer_count), channels)
-    return pl.pallas_call(
+    depth, channels = weight.shape
+    width = tokens // (2 * outer_count)
+    part = (outer_count, width, channels)
+    estimate = pl.CostEstimate(
+        flops=tokens * depth * channels,
+        bytes_accessed=2 * weight.size + 3 * tokens * channels,
+        transcendentals=0,
+    )
+    send, rest = pl.pallas_call(
         functools.partial(
-            spread_kernel, places=places, frames_axis=frames_axis, rows_axis=rows_axis
+            spread_kernel, places=places, parity_axes=parity_axes, rows_axis=rows_axis
         ),
         out_shape=[
             jax.ShapeDtypeStruct(part, jnp.bfloat16),
-            jax.ShapeDtypeStruct(part, jnp.float32),
+            jax.ShapeDtypeStruct((outer_count, width, depth), jnp.bfloat16),
         ],
         in_specs=[pl.BlockSpec(memory_space=pltpu.VMEM)] * (len(pieces) + 1),
         out_specs=[pl.BlockSpec(memory_space=pltpu.VMEM)] * 2,
         scratch_shapes=[
-            pltpu.VMEM((len(pieces) * k, tokens), jnp.bfloat16),
-            pltpu.VMEM((2,) + part, jnp.float32),
+            pltpu.VMEM((depth, tokens), jnp.bfloat16),
+            pltpu.VMEM((2 * outer_count, width, depth), jnp.bfloat16),
         ],
         compiler_params=pltpu.CompilerParams(vmem_limit_bytes=VMEM_LIMIT),
-        cost_estimate=pl.CostEstimate(
-            flops=2 * len(pieces) * tokens * k * channels,
-            bytes_accessed=2 * weight.size + 6 * tokens * channels,
-            transcendentals=0,
-        ),
+        cost_estimate=estimate,
     )(*pieces, weight)
+    keep = pl.pallas_call(
+        keep_kernel,
+        out_shape=jax.ShapeDtypeStruct(part, jnp.float32),
+        in_specs=[pl.BlockSpec(memory_space=pltpu.VMEM)] * 2,
+        out_specs=pl.BlockSpec(memory_space=pltpu.VMEM),
+        compiler_params=pltpu.CompilerParams(vmem_limit_bytes=VMEM_LIMIT),
+        cost_estimate=estimate,
+    )(rest, weight)
+    return send, keep
 
 
 def merge_kernel(mine_ref, theirs_ref, *refs, axis, inner_count):
@@ -344,37 +358,36 @@
         groups = [pairs[i : i + parts] for i in range(0, len(pairs), parts)]
         keys = [wide(key for key, _ in group) for group in groups]
         values = [wide(value for _, value in group) for group in groups]
-        asked = (wide(q[head] for q in own_q), wide(qkv[0, head] for qkv in pair_qkv))
-        for which, query in enumerate(asked):
-            query = (query.astype(jnp.float32) * scale).astype(jnp.bfloat16)
-            scores = [
-                lax.dot_general(key, query, contract_first, preferred_element_type=jnp.float32)
-                for key in keys
-            ]
-            peak = functools.reduce(
-                jnp.maximum, [jnp.max(s, axis=0, keepdims=True) for s in scores]
+        asked = [q[head] for q in own_q] + [qkv[0, head] for qkv in pair_qkv]
+        query = (wide(asked).astype(jnp.float32) * scale).astype(jnp.bfloat16)
+        scores = [
+            lax.dot_general(key, query, contract_first, preferred_element_type=jnp.float32)
+            for key in keys
+        ]
+        peak = functools.reduce(jnp.maximum, [jnp.max(s, axis=0, keepdims=True) for s in scores])
+        if first:
+            denominator = jnp.zeros_like(peak)
+            numerator = jnp.zeros((HD, query.shape[1]), jnp.float32)
+        else:
+            old_peak, denominator, numerator = (ref[head] for ref in state)
+            peak = jnp.maximum(peak, old_peak)
+            shrink = jnp.exp(old_peak - peak)
+            denominator, numerator = denominator * shrink, numerator * shrink
+        for value, score in zip(values, scores):
+            weights = jnp.exp(score - peak)
+            denominator = denominator + jnp.sum(weights, axis=0, keepdims=True)
+            numerator = numerator + jnp.dot(
+                value, weights.astype(jnp.bfloat16), preferred_element_type=jnp.float32
             )
-            if first:
-                denominator = jnp.zeros_like(peak)
-                numerator = jnp.zeros((HD, query.shape[1]), jnp.float32)
-            else:
-                old_peak, denominator, numerator = (ref[head, which] for ref in state)
-                peak = jnp.maximum(peak, old_peak)
-                shrink = jnp.exp(old_peak - peak)
-                denominator, numerator = denominator * shrink, numerator * shrink
-            for value, score in zip(values, scores):
-                weights = jnp.exp(score - peak)
-                denominator = denominator + jnp.sum(weights, axis=0, keepdims=True)
-                numerator = numerator + jnp.dot(
-                    value, weights.astype(jnp.bfloat16), preferred_element_type=jnp.float32
-                )
-            if last:
-                out = outs[which]
-                result = (numerator / denominator).T
-                out[:, head * HD : (head + 1) * HD] = result.astype(out.dtype)
-            else:
-                for ref, value in zip(outs, (peak, denominator, numerator)):
-                    ref[head, which] = value
+        if last:
+            result = (numerator / denominator).T
+            tokens = outs[0].shape[0]
+            for which, out in enumerate(outs):
+                mine = result[which * tokens : (which + 1) * tokens]
+                out[:, head * HD : (head + 1) * HD] = mine.astype(out.dtype)
+        else:
+            for ref, value in zip(outs, (peak, denominator, numerator)):
+                ref[head] = value
 
 
 def attend(own_q, pair_qkv, kvs, state, last):
@@ -386,7 +399,7 @@
         shapes = [jax.ShapeDtypeStruct((tokens, heads * HD), jnp.bfloat16)] * 2
     else:
         shapes = [
-            jax.ShapeDtypeStruct((heads, 2, rows, tokens), jnp.float32) for rows in (1, 1, HD)
+            jax.ShapeDtypeStruct((heads, rows, 2 * tokens), jnp.float32) for rows in (1, 1, HD)
         ]
     work = 2 * heads * tokens * keys
     args = (*own_q, *kvs, *pair_qkv, *state)
@@ -458,42 +471,44 @@
         ((1, 1), (2, 0), (0, 2)),
         temporal_weight.reshape(3 * local_out, channels),
         outer_size,
-        "frames",
+        ("frames",),
         "rows",
     )
     sends, keeps = merge(chip_sum, swap(send, "rows", 1), "rows", inner_size)
     sends, weights = lax.optimization_barrier((sends, weights))
-    weights[inner_size + 1] = swap(weights[inner_size], "rows", 1)
     others = [swap(sends[1 - mask], "rows", inner_size) for mask in range(outer_size)]
+    tokens = []
+    for mask in range(outer_size):
+        normed, *wanted = norm_of_hidden(
+            pieces[mask * inner_size],
+            keeps[mask],
+            others[mask],
+            temporal_bias,
+            token_gain,
+            mask == 0,
+        )
+        hidden = wanted[0] if wanted else hidden
+        tokens.append([normed, swap(normed, "rows", 1)])
+        tokens[0], others = lax.optimization_barrier((tokens[0], others))
     own_q, own_kv, pair_qkv, far = [], [], [], []
     for mask in range(outer_size):
-        latent_rows, other = pieces[mask * inner_size], others[mask]
-        if mask:
-            other, weights = lax.optimization_barrier((other, weights))
-        normed, *wanted = norm_of_hidden(
-            latent_rows, keeps[mask], other, temporal_bias, token_gain, mask == 0
-        )
-        hidden = wanted[0] if wanted else hidden
         q, kv, *sent = project(
-            [normed, swap(normed, "rows", 1)],
-            query_weight,
-            key_weight,
-            value_weight,
-            "frames",
-            "rows",
+            tokens[mask], query_weight, key_weight, value_weight, "frames", "rows"
         )
         own_q.append(q)
         own_kv.append(kv)
         far.append(
             [
                 swap(sent[1] if m % 2 else kv, "frames", m)
-                for m in range(frames_size - 1, 1, -1)
+                for m in range(2, frames_size)
             ]
         )
         pair_qkv.append(swap(sent[0], "frames", 1))
     early, late = own_kv + far[0][:1], far[0][1:] + far[1]
     state = attend(own_q, pair_qkv, early, (), not late)
     own_out, pair_out = attend(own_q, pair_qkv, late, state, True) if late else state
+    own_out, pair_out, weights = lax.optimization_barrier((own_out, pair_out, weights))
+    weights[inner_size + 1] = swap(weights[inner_size], "rows", 1)
     dealt = deal(own_out, pair_out, rows_size, "frames", "rows", inner_size)
     together = 2 * rows_size
     groups = [

time: 64.5 us -> 62.7 us (0.972)
  waiting for transfers between devices: 21.4 us -> 20.1 us
    ppermute x17, waiting for transfers between devices: 17.1 us -> 15.7 us  [swap(): return lax.ppermute(array, axis, [(i, i ^ stride) for i in range(size)])]
    pallas_call x2, Pallas kernels: 3.24 us -> 2.58 us  [attend(): pl.pallas_call(functools.partial(attention_kernel, parts=parts, kv_count=...]
  transfers between devices with their start and end apart: 19 -> 19, of which waited for: 9 -> 10; matrix products, arithmetic and copies ran while one was open for 0% -> 0% of each run, Pallas kernels for 12% -> 12%
where the time goes in v2:
time: 62.7 us; the launch traced here: 62.5 us
  starting transfers between devices  21.2 us (34%)
  waiting for transfers between devices  20.1 us (32%)
  Pallas kernels  10 us (16%)
  blocking collectives  7.81 us (12%)
  local copies, waits for them, and re-layouts  3.15 us (5%)
    ppermute x17, starting transfers between devices, swap(): return lax.ppermute(array, axis, [(i, i ^ stride) for i in range(size)])  16 us
    ppermute x17, waiting for transfers between devices, swap(): return lax.ppermute(array, axis, [(i, i ^ stride) for i in range(size)])  15.7 us
    all_to_all x1, blocking collectives, body(): lax.all_to_all(dealt.reshape((together,) + dealt.shape[2:]), ('frames', '...  7.81 us
    ppermute x2, starting transfers between devices, neighbours(): return (lax.ppermute(array, axis, even), lax.ppermute(array, axis, odd))  5.13 us
    ppermute x2, waiting for transfers between devices, neighbours(): return (lax.ppermute(array, axis, even), lax.ppermute(array, axis, odd))  4.37 us
    unnamed x24, local copies, waits for them, and re-layouts  3.15 us
    pallas_call x2, Pallas kernels, attend(): pl.pallas_call(functools.partial(attention_kernel, parts=parts, kv_count=...  2.58 us
    pallas_call x1, Pallas kernels, conv_norm(): pl.pallas_call(functools.partial(conv_kernel, pieces=len(pieces), cols=co...  2.56 us
  transfers between devices with their start and end apart: 19, of which 10 were waited for; matrix products, arithmetic and copies ran while one was open for 0% of the time, Pallas kernels for 12%

profile of v2, /device:TPU:0, one launch (start us, length us, event | category | flops | bytes accessed | tf_op | source)
XLA Modules:
  0.0 62.5 jit_solution(5424936821934640432)
XLA Ops:
  0.0 2.9 %collective-permute-start.1 = (bf16[64,1280]{1,0:T(8,128)(2,1)}, bf16[64,1280]{1,0:T(8,128)(2,1)S(1)}, u32[]{:S(2)}, u32[]{:S(2)}) collective-permute-start(bf16[64,1280]{1,0:T(8,128)(2,1)} %bitcast.11), channel_id=1, source_target_pairs={{0,2},{1,3},{2,0},{3,1},{4,6},{5,7},{6,4},{7,5},{8,10},{9,11},{10,... | collective-permute-start | bytes 491528 | tf_op jit(solution)/shard_map/ppermute | solution.py:18
  2.9 3.1 %copy-done.1 = bf16[3,3,1280,320]{2,3,1,0:T(8,128)(2,1)S(1)} copy-done((bf16[3,3,1280,320]{2,3,1,0:T(8,128)(2,1)S(1)}, bf16[3,3,1280,320]{2,3,1,0:T(8,128)(2,1)}, u32[]{:S(2)}) %copy-start.1) | copy-done | bytes 7372824
  6.1 0.6 shard_map.118.refs_4_
  6.7 0.7 %collective-permute-done.1.refs_2_.latents_ref = bf16[64,1280]{1,0:T(8,128)(2,1)S(1)} collective-permute-done((bf16[64,1280]{1,0:T(8,128)(2,1)}, bf16[64,1280]{1,0:T(8,128)(2,1)S(1)}, u32[]{:S(2)}, u32[]{:S(2)}) %collective-permute-start.1) | collective-permute-done | bytes 163872 | tf_op jit(solution)/shard_map/ppermute | solution.py:18
  7.4 1.7 %collective-permute-start.7 = (bf16[256,1280]{1,0:T(8,128)(2,1)S(1)}, bf16[256,1280]{1,0:T(8,128)(2,1)S(1)}, u32[]{:S(2)}, u32[]{:S(2)}) collective-permute-start(bf16[256,1280]{1,0:T(8,128)(2,1)S(1)} %copy-done.5), channel_id=1, source_target_pairs={{0,2},{1,3},{2,0},{3,1},{4,6},{5,7},{6,4},{7,5},{8,10},{9,11},{10,... | collective-permute-start | bytes 1966088 | tf_op jit(solution)/shard_map/ppermute | solution.py:18
  9.4 2.6 %shard_map.119.refs_0_ = bf16[320,256]{1,0:T(8,128)(2,1)S(1)} custom-call(bf16[64,1280]{1,0:T(8,128)(2,1)S(1)} %bitcast.13, bf16[64,1280]{1,0:T(8,128)(2,1)S(1)} %collective-permute-done.refs_1_, bf16[64,1280]{1,0:T(8,128)(2,1)S(1)} %collective-permute-done.1.refs_2_.latents_ref, bf16[64,1280]{1,0:T(8,128)(2,1)S(1)} %collective-permute-done.2.refs_3_, ...), custom_call_target="tpu_custom_call" | custom-call | flops 1887436800 | bytes 8192000 | tf_op jit(solution)/shard_map/pallas_call | solution.py:104
  11.9 0.7 %collective-permute-start.4 = (bf16[320,256]{1,0:T(8,128)(2,1)S(1)}, bf16[320,256]{1,0:T(8,128)(2,1)S(1)}, u32[]{:S(2)}, u32[]{:S(2)}) collective-permute-start(bf16[320,256]{1,0:T(8,128)(2,1)S(1)} %shard_map.119.refs_0_), channel_id=1, source_target_pairs={{4,8},{8,4},{5,9},{9,5},{6,10},{10,6},{7,11},{11,7},{20,24},{24,20... | collective-permute-start | bytes 491528 | tf_op jit(solution)/shard_map/ppermute | solution.py:25
  12.6 4.5 %collective-permute-start.3 = (bf16[320,256]{1,0:T(8,128)(2,1)S(1)}, bf16[320,256]{1,0:T(8,128)(2,1)S(1)}, u32[]{:S(2)}, u32[]{:S(2)}) collective-permute-start(bf16[320,256]{1,0:T(8,128)(2,1)S(1)} %shard_map.119.refs_0_), channel_id=1, source_target_pairs={{0,4},{4,0},{8,12},{12,8},{1,5},{5,1},{9,13},{13,9},{2,6},{6,2},{1... | collective-permute-start | bytes 491528 | tf_op jit(solution)/shard_map/ppermute | solution.py:25
  17.1 4.4 %collective-permute-done.3.refs_1_ = bf16[320,256]{1,0:T(8,128)(2,1)S(1)} collective-permute-done((bf16[320,256]{1,0:T(8,128)(2,1)S(1)}, bf16[320,256]{1,0:T(8,128)(2,1)S(1)}, u32[]{:S(2)}, u32[]{:S(2)}) %collective-permute-start.3) | collective-permute-done | bytes 163872 | tf_op jit(solution)/shard_map/ppermute | solution.py:25
  21.4 0.7 %shard_map.120 = (bf16[2,64,1280]{2,1,0:T(8,128)(2,1)S(1)}, bf16[2,64,960]{2,1,0:T(8,128)(2,1)S(1)}) custom-call(bf16[320,256]{1,0:T(8,128)(2,1)S(1)} %shard_map.119.refs_0_, bf16[320,256]{1,0:T(8,128)(2,1)S(1)} %collective-permute-done.3.refs_1_, bf16[320,256]{1,0:T(8,128)(2,1)S(1)} %collective-permute-done.4.refs_2_, bf16[960,1280]{1,0:T(8,128)(2,1)S(1)} %bitcast.8), custom_call_target="tpu_custom_call" | custom-call | flops 314572800 | bytes 3440640 | tf_op jit(solution)/shard_map/pallas_call | solution.py:158
  22.2 0.5 shard_map.121.mine_ref
  22.8 1.1 %collective-permute-done.5.theirs_ref = bf16[2,64,1280]{2,1,0:T(8,128)(2,1)S(1)} collective-permute-done((bf16[2,64,1280]{2,1,0:T(8,128)(2,1)S(1)}, bf16[2,64,1280]{2,1,0:T(8,128)(2,1)S(1)}, u32[]{:S(2)}, u32[]{:S(2)}) %collective-permute-start.5) | collective-permute-done | bytes 327712 | tf_op jit(solution)/shard_map/ppermute | solution.py:18
  23.9 0.6 collective-permute-done.7.refs_2_
  24.5 1.7 %collective-permute-start.8 = (bf16[64,1280]{1,0:T(8,128)(2,1)S(1)}, bf16[64,1280]{1,0:T(8,128)(2,1)S(1)}, u32[]{:S(2)}, u32[]{:S(2)}) collective-permute-start(bf16[64,1280]{1,0:T(8,128)(2,1)S(1)} %get-tuple-element.54), channel_id=1, source_target_pairs={{0,2},{1,3},{2,0},{3,1},{4,6},{5,7},{6,4},{7,5},{8,10},{9,11},{10,... | collective-permute-start | bytes 491528 | tf_op jit(solution)/shard_map/ppermute | solution.py:18
  26.2 0.3 collective-permute-start.10
  26.5 5.1 %collective-permute-done.8.theirs_ref = bf16[64,1280]{1,0:T(8,128)(2,1)S(1)} collective-permute-done((bf16[64,1280]{1,0:T(8,128)(2,1)S(1)}, bf16[64,1280]{1,0:T(8,128)(2,1)S(1)}, u32[]{:S(2)}, u32[]{:S(2)}) %collective-permute-start.8) | collective-permute-done | bytes 163872 | tf_op jit(solution)/shard_map/ppermute | solution.py:18
  32.0 1.9 %collective-permute-done.10.theirs_ref = bf16[64,1280]{1,0:T(8,128)(2,1)S(1)} collective-permute-done((bf16[64,1280]{1,0:T(8,128)(2,1)S(1)}, bf16[64,1280]{1,0:T(8,128)(2,1)S(1)}, u32[]{:S(2)}, u32[]{:S(2)}) %collective-permute-start.10) | collective-permute-done | bytes 163872 | tf_op jit(solution)/shard_map/ppermute | solution.py:18
  34.2 0.6 shard_map.124
  34.8 2.9 %collective-permute-start.17 = (bf16[2,2,64,128]{3,2,1,0:T(8,128)(2,1)S(1)}, bf16[2,2,64,128]{3,2,1,0:T(8,128)(2,1)S(1)}, u32[]{:S(2)}, u32[]{:S(2)}) collective-permute-start(bf16[2,2,64,128]{3,2,1,0:T(8,128)(2,1)S(1)} %get-tuple-element.70.refs_2_), channel_id=1, source_target_pairs={{0,8},{4,12},{8,0},{12,4},{1,9},{5,13},{9,1},{13,5},{2,10},{6,14},... | collective-permute-start | bytes 196616 | tf_op jit(solution)/shard_map/ppermute | solution.py:18
  37.7 1.6 %collective-permute-start.15 = (bf16[3,2,64,128]{3,2,1,0:T(8,128)(2,1)S(1)}, bf16[3,2,64,128]{3,2,1,0:T(8,128)(2,1)S(1)}, u32[]{:S(2)}, u32[]{:S(2)}) collective-permute-start(bf16[3,2,64,128]{3,2,1,0:T(8,128)(2,1)S(1)} %get-tuple-element.68), channel_id=1, source_target_pairs={{0,4},{4,0},{8,12},{12,8},{1,5},{5,1},{9,13},{13,9},{2,6},{6,2},{1... | collective-permute-start | bytes 294920 | tf_op jit(solution)/shard_map/ppermute | solution.py:18
  39.3 0.6 shard_map.126
  39.9 0.5 collective-permute-start.16
  40.4 1.3 %collective-permute-start.12 = (bf16[2,2,64,128]{3,2,1,0:T(8,128)(2,1)S(1)}, bf16[2,2,64,128]{3,2,1,0:T(8,128)(2,1)S(1)}, u32[]{:S(2)}, u32[]{:S(2)}) collective-permute-start(bf16[2,2,64,128]{3,2,1,0:T(8,128)(2,1)S(1)} %get-tuple-element.65), channel_id=1, source_target_pairs={{0,12},{4,8},{8,4},{12,0},{1,13},{5,9},{9,5},{13,1},{2,14},{6,10},... | collective-permute-start | bytes 196616 | tf_op jit(solution)/shard_map/ppermute | solution.py:18
  41.8 2.5 %collective-permute-start.14 = (bf16[2,2,64,128]{3,2,1,0:T(8,128)(2,1)S(1)}, bf16[2,2,64,128]{3,2,1,0:T(8,128)(2,1)S(1)}, u32[]{:S(2)}, u32[]{:S(2)}) collective-permute-start(bf16[2,2,64,128]{3,2,1,0:T(8,128)(2,1)S(1)} %get-tuple-element.67), channel_id=1, source_target_pairs={{0,12},{4,8},{8,4},{12,0},{1,13},{5,9},{9,5},{13,1},{2,14},{6,10},... | collective-permute-start | bytes 196616 | tf_op jit(solution)/shard_map/ppermute | solution.py:18
  44.3 0.7 %collective-permute-done.16.refs_6_ = bf16[3,2,64,128]{3,2,1,0:T(8,128)(2,1)S(1)} collective-permute-done((bf16[3,2,64,128]{3,2,1,0:T(8,128)(2,1)S(1)}, bf16[3,2,64,128]{3,2,1,0:T(8,128)(2,1)S(1)}, u32[]{:S(2)}, u32[]{:S(2)}) %collective-permute-start.16) | collective-permute-done | bytes 98336 | tf_op jit(solution)/shard_map/ppermute | solution.py:18
  45.0 1.4 %shard_map.127 = (f32[2,1,512]{2,1,0:T(1,128)S(1)}, f32[2,1,512]{2,1,0:T(1,128)S(1)}, f32[2,64,512]{2,1,0:T(8,128)S(1)}) custom-call(bf16[2,64,128]{2,1,0:T(8,128)(2,1)S(1)} %get-tuple-element.61.refs_0_, bf16[2,64,128]{2,1,0:T(8,128)(2,1)S(1)} %get-tuple-element.64.refs_1_, bf16[2,2,64,128]{3,2,1,0:T(8,128)(2,1)S(1)} %get-tuple-element.70.refs_2_, ...), custom_call_target="tpu_custom_call" | custom-call | flops 167772160 | bytes 458752 | tf_op jit(solution)/shard_map/pallas_call | solution.py:406
  46.4 1.3 %collective-permute-done.12.refs_2_ = bf16[2,2,64,128]{3,2,1,0:T(8,128)(2,1)S(1)} collective-permute-done((bf16[2,2,64,128]{3,2,1,0:T(8,128)(2,1)S(1)}, bf16[2,2,64,128]{3,2,1,0:T(8,128)(2,1)S(1)}, u32[]{:S(2)}, u32[]{:S(2)}) %collective-permute-start.12) | collective-permute-done | bytes 65568 | tf_op jit(solution)/shard_map/ppermute | solution.py:18
  47.7 1.4 %collective-permute-done.14.refs_4_ = bf16[2,2,64,128]{3,2,1,0:T(8,128)(2,1)S(1)} collective-permute-done((bf16[2,2,64,128]{3,2,1,0:T(8,128)(2,1)S(1)}, bf16[2,2,64,128]{3,2,1,0:T(8,128)(2,1)S(1)}, u32[]{:S(2)}, u32[]{:S(2)}) %collective-permute-start.14) | collective-permute-done | bytes 65568 | tf_op jit(solution)/shard_map/ppermute | solution.py:18
  49.1 3.0 %collective-permute-done.13.refs_3_ = bf16[2,2,64,128]{3,2,1,0:T(8,128)(2,1)S(1)} collective-permute-done((bf16[2,2,64,128]{3,2,1,0:T(8,128)(2,1)S(1)}, bf16[2,2,64,128]{3,2,1,0:T(8,128)(2,1)S(1)}, u32[]{:S(2)}, u32[]{:S(2)}) %collective-permute-start.13) | collective-permute-done | bytes 65568 | tf_op jit(solution)/shard_map/ppermute | solution.py:18
  52.1 1.2 %shard_map.128 = (bf16[256,128]{1,0:T(8,128)(2,1)S(1)}, bf16[256,128]{1,0:T(8,128)(2,1)S(1)}) custom-call(bf16[2,64,128]{2,1,0:T(8,128)(2,1)S(1)} %get-tuple-element.61.refs_0_, bf16[2,64,128]{2,1,0:T(8,128)(2,1)S(1)} %get-tuple-element.64.refs_1_, bf16[2,2,64,128]{3,2,1,0:T(8,128)(2,1)S(1)} %collective-permute-done.12.refs_2_, ...), custom_call_target="tpu_custom_call" | custom-call | flops 100663296 | bytes 729088 | tf_op jit(solution)/shard_map/pallas_call | solution.py:406
  53.4 7.8 %all_to_all.5 = bf16[8,64,128]{2,1,0:T(8,128)(2,1)S(1)} all-to-all(bf16[8,64,128]{2,1,0:T(8,128)(2,1)S(1)} %bitcast.16), channel_id=1, replica_groups={{0,1,2,3,4,5,6,7},{8,9,10,11,12,13,14,15},{16,17,18,19,20,21,22,23},{24..., dimensions={0} | all-to-all | bytes 262144 | tf_op jit(solution)/shard_map/all_to_all | solution.py:518
  61.3 1.2 %shard_map.130 = bf16[64,1280]{1,0:T(8,128)(2,1)} custom-call(bf16[2,4,64,128]{3,2,1,0:T(8,128)(2,1)S(1)} %bitcast.15, bf16[256,1280]{1,0:T(8,128)(2,1)S(1)} %copy-done.5, bf16[256,1280]{1,0:T(8,128)(2,1)S(1)} %collective-permute-done.6.refs_1_, bf16[256,1280]{1,0:T(8,128)(2,1)S(1)} %collective-permute-done.7.refs_2_, ...), custom_call_target="tpu_custom_call" | custom-call | flops 167772160 | bytes 2949120 | tf_op jit(solution)/shard_map/pallas_call | solution.py:250
  (44 shorter events, 1.3 us)
Async XLA Ops:
  0.0 7.3 %collective-permute-start.1 = (bf16[64,1280]{1,0:T(8,128)(2,1)}, bf16[64,1280]{1,0:T(8,128)(2,1)S(1)}, u32[]{:S(2)}, u32[]{:S(2)}) collective-permute-start(bf16[64,1280]{1,0:T(8,128)(2,1)} %bitcast.11), channel_id=1, source_target_pairs={{0,2},{1,3},{2,0},{3,1},{4,6},{5,7},{6,4},{7,5},{8,10},{9,11},{10,... | collective-permute-start | bytes 491528 | tf_op jit(solution)/shard_map/ppermute | solution.py:18
  2.9 6.4 %collective-permute-start = (bf16[64,1280]{1,0:T(8,128)(2,1)}, bf16[64,1280]{1,0:T(8,128)(2,1)S(1)}, u32[]{:S(2)}, u32[]{:S(2)}) collective-permute-start(bf16[64,1280]{1,0:T(8,128)(2,1)} %bitcast.12), channel_id=1, source_target_pairs={{0,1},{1,0},{2,3},{3,2},{4,5},{5,4},{6,7},{7,6},{8,9},{9,8},{10,11... | collective-permute-start | bytes 491528 | tf_op jit(solution)/shard_map/ppermute | solution.py:18
  2.9 3.1 %copy-start.1 = (bf16[3,3,1280,320]{2,3,1,0:T(8,128)(2,1)S(1)}, bf16[3,3,1280,320]{2,3,1,0:T(8,128)(2,1)}, u32[]{:S(2)}) copy-start(bf16[3,3,1280,320]{2,3,1,0:T(8,128)(2,1)} %param.13) | copy-start | bytes 22118404
  6.0 1.3 %copy-start.5 = (bf16[256,1280]{1,0:T(8,128)(2,1)S(1)}, bf16[256,1280]{1,0:T(8,128)(2,1)}, u32[]{:S(2)}) copy-start(bf16[256,1280]{1,0:T(8,128)(2,1)} %refs_0_) | copy-start | bytes 1966084
  6.0 3.3 %copy-start.6 = (bf16[4,1,16,1280]{3,2,1,0:T(8,128)(2,1)S(1)}, bf16[4,1,16,1280]{3,2,1,0:T(8,128)(2,1)}, u32[]{:S(2)}) copy-start(bf16[4,1,16,1280]{3,2,1,0:T(8,128)(2,1)} %param.12) | copy-start | bytes 491524
  6.0 3.3 %copy-start.9 = (f32[320]{0:T(512)S(1)}, f32[320]{0:T(512)}, u32[]{:S(2)}) copy-start(f32[320]{0:T(512)} %refs_5_.1) | copy-start | bytes 3844
  6.0 3.3 %copy-start.10 = (f32[320]{0:T(512)S(1)}, f32[320]{0:T(512)}, u32[]{:S(2)}) copy-start(f32[320]{0:T(512)} %refs_6_.1) | copy-start | bytes 3844
  6.0 3.3 %copy-start.11 = (f32[320]{0:T(512)S(1)}, f32[320]{0:T(512)}, u32[]{:S(2)}) copy-start(f32[320]{0:T(512)} %refs_7_.1) | copy-start | bytes 3844
  6.6 14.8 %copy-start = (bf16[3,320,1280]{2,1,0:T(8,128)(2,1)S(1)}, bf16[3,320,1280]{2,1,0:T(8,128)(2,1)}, u32[]{:S(2)}) copy-start(bf16[3,320,1280]{2,1,0:T(8,128)(2,1)} %param.17) | copy-start | bytes 7372804
  6.6 25.0 %copy-start.7 = (f32[1280]{0:T(1024)S(1)}, f32[1280]{0:T(1024)}, u32[]{:S(2)}) copy-start(f32[1280]{0:T(1024)} %bias_ref.3) | copy-start | bytes 15364
  6.6 25.0 %copy-start.8 = (f32[1280]{0:T(1024)S(1)}, f32[1280]{0:T(1024)}, u32[]{:S(2)}) copy-start(f32[1280]{0:T(1024)} %gain_ref.3) | copy-start | bytes 15364
  6.7 27.6 %copy-start.2 = (bf16[1280,256]{1,0:T(8,128)(2,1)S(1)}, bf16[1280,256]{1,0:T(8,128)(2,1)}, u32[]{:S(2)}) copy-start(bf16[1280,256]{1,0:T(8,128)(2,1)} %refs_2_.3) | copy-start | bytes 1966084
  6.7 27.6 %copy-start.3 = (bf16[1280,256]{1,0:T(8,128)(2,1)S(1)}, bf16[1280,256]{1,0:T(8,128)(2,1)}, u32[]{:S(2)}) copy-start(bf16[1280,256]{1,0:T(8,128)(2,1)} %refs_3_.3) | copy-start | bytes 1966084
  6.7 27.6 %copy-start.4 = (bf16[1280,256]{1,0:T(8,128)(2,1)S(1)}, bf16[1280,256]{1,0:T(8,128)(2,1)}, u32[]{:S(2)}) copy-start(bf16[1280,256]{1,0:T(8,128)(2,1)} %refs_4_.3) | copy-start | bytes 1966084
  7.3 2.0 %collective-permute-start.2 = (bf16[64,1280]{1,0:T(8,128)(2,1)S(1)}, bf16[64,1280]{1,0:T(8,128)(2,1)S(1)}, u32[]{:S(2)}, u32[]{:S(2)}) collective-permute-start(bf16[64,1280]{1,0:T(8,128)(2,1)S(1)} %collective-permute-done.1.refs_2_.latents_ref), channel_id=1, source_target_pairs={{0,1},{1,0},{2,3},{3,2},{4,5},{5,4},{6,7},{7,6},{8,9},{9,8},{10,11... | collective-permute-start | bytes 491528 | tf_op jit(solution)/shard_map/ppermute | solution.py:18
  7.4 17.1 %collective-permute-start.7 = (bf16[256,1280]{1,0:T(8,128)(2,1)S(1)}, bf16[256,1280]{1,0:T(8,128)(2,1)S(1)}, u32[]{:S(2)}, u32[]{:S(2)}) collective-permute-start(bf16[256,1280]{1,0:T(8,128)(2,1)S(1)} %copy-done.5), channel_id=1, source_target_pairs={{0,2},{1,3},{2,0},{3,1},{4,6},{5,7},{6,4},{7,5},{8,10},{9,11},{10,... | collective-permute-start | bytes 1966088 | tf_op jit(solution)/shard_map/ppermute | solution.py:18
  9.1 15.4 %collective-permute-start.6 = (bf16[256,1280]{1,0:T(8,128)(2,1)S(1)}, bf16[256,1280]{1,0:T(8,128)(2,1)S(1)}, u32[]{:S(2)}, u32[]{:S(2)}) collective-permute-start(bf16[256,1280]{1,0:T(8,128)(2,1)S(1)} %copy-done.5), channel_id=1, source_target_pairs={{0,1},{1,0},{2,3},{3,2},{4,5},{5,4},{6,7},{7,6},{8,9},{9,8},{10,11... | collective-permute-start | bytes 1966088 | tf_op jit(solution)/shard_map/ppermute | solution.py:18
  11.9 5.1 %collective-permute-start.4 = (bf16[320,256]{1,0:T(8,128)(2,1)S(1)}, bf16[320,256]{1,0:T(8,128)(2,1)S(1)}, u32[]{:S(2)}, u32[]{:S(2)}) collective-permute-start(bf16[320,256]{1,0:T(8,128)(2,1)S(1)} %shard_map.119.refs_0_), channel_id=1, source_target_pairs={{4,8},{8,4},{5,9},{9,5},{6,10},{10,6},{7,11},{11,7},{20,24},{24,20... | collective-permute-start | bytes 491528 | tf_op jit(solution)/shard_map/ppermute | solution.py:25
  12.6 8.8 %collective-permute-start.3 = (bf16[320,256]{1,0:T(8,128)(2,1)S(1)}, bf16[320,256]{1,0:T(8,128)(2,1)S(1)}, u32[]{:S(2)}, u32[]{:S(2)}) collective-permute-start(bf16[320,256]{1,0:T(8,128)(2,1)S(1)} %shard_map.119.refs_0_), channel_id=1, source_target_pairs={{0,4},{4,0},{8,12},{12,8},{1,5},{5,1},{9,13},{13,9},{2,6},{6,2},{1... | collective-permute-start | bytes 491528 | tf_op jit(solution)/shard_map/ppermute | solution.py:25
  22.2 1.7 %collective-permute-start.5 = (bf16[2,64,1280]{2,1,0:T(8,128)(2,1)S(1)}, bf16[2,64,1280]{2,1,0:T(8,128)(2,1)S(1)}, u32[]{:S(2)}, u32[]{:S(2)}) collective-permute-start(bf16[2,64,1280]{2,1,0:T(8,128)(2,1)S(1)} %get-tuple-element.49), channel_id=1, source_target_pairs={{0,1},{1,0},{2,3},{3,2},{4,5},{5,4},{6,7},{7,6},{8,9},{9,8},{10,11... | collective-permute-start | bytes 983048 | tf_op jit(solution)/shard_map/ppermute | solution.py:18
  24.5 7.1 %collective-permute-start.8 = (bf16[64,1280]{1,0:T(8,128)(2,1)S(1)}, bf16[64,1280]{1,0:T(8,128)(2,1)S(1)}, u32[]{:S(2)}, u32[]{:S(2)}) collective-permute-start(bf16[64,1280]{1,0:T(8,128)(2,1)S(1)} %get-tuple-element.54), channel_id=1, source_target_pairs={{0,2},{1,3},{2,0},{3,1},{4,6},{5,7},{6,4},{7,5},{8,10},{9,11},{10,... | collective-permute-start | bytes 491528 | tf_op jit(solution)/shard_map/ppermute | solution.py:18
  26.2 7.6 %collective-permute-start.10 = (bf16[64,1280]{1,0:T(8,128)(2,1)S(1)}, bf16[64,1280]{1,0:T(8,128)(2,1)S(1)}, u32[]{:S(2)}, u32[]{:S(2)}) collective-permute-start(bf16[64,1280]{1,0:T(8,128)(2,1)S(1)} %get-tuple-element.56), channel_id=1, source_target_pairs={{0,2},{1,3},{2,0},{3,1},{4,6},{5,7},{6,4},{7,5},{8,10},{9,11},{10,... | collective-permute-start | bytes 491528 | tf_op jit(solution)/shard_map/ppermute | solution.py:18
  31.9 2.0 %collective-permute-start.9 = (bf16[64,1280]{1,0:T(8,128)(2,1)S(1)}, bf16[64,1280]{1,0:T(8,128)(2,1)S(1)}, u32[]{:S(2)}, u32[]{:S(2)}) collective-permute-start(bf16[64,1280]{1,0:T(8,128)(2,1)S(1)} %get-tuple-element.59.refs_0_), channel_id=1, source_target_pairs={{0,1},{1,0},{2,3},{3,2},{4,5},{5,4},{6,7},{7,6},{8,9},{9,8},{10,11... | collective-permute-start | bytes 491528 | tf_op jit(solution)/shard_map/ppermute | solution.py:18
  34.1 5.2 %collective-permute-start.11 = (bf16[64,1280]{1,0:T(8,128)(2,1)S(1)}, bf16[64,1280]{1,0:T(8,128)(2,1)S(1)}, u32[]{:S(2)}, u32[]{:S(2)}) collective-permute-start(bf16[64,1280]{1,0:T(8,128)(2,1)S(1)} %shard_map.125.refs_0_), channel_id=1, source_target_pairs={{0,1},{1,0},{2,3},{3,2},{4,5},{5,4},{6,7},{7,6},{8,9},{9,8},{10,11... | collective-permute-start | bytes 491528 | tf_op jit(solution)/shard_map/ppermute | solution.py:18
  34.8 9.4 %collective-permute-start.17 = (bf16[2,2,64,128]{3,2,1,0:T(8,128)(2,1)S(1)}, bf16[2,2,64,128]{3,2,1,0:T(8,128)(2,1)S(1)}, u32[]{:S(2)}, u32[]{:S(2)}) collective-permute-start(bf16[2,2,64,128]{3,2,1,0:T(8,128)(2,1)S(1)} %get-tuple-element.70.refs_2_), channel_id=1, source_target_pairs={{0,8},{4,12},{8,0},{12,4},{1,9},{5,13},{9,1},{13,5},{2,10},{6,14},... | collective-permute-start | bytes 196616 | tf_op jit(solution)/shard_map/ppermute | solution.py:18
  37.7 6.5 %collective-permute-start.15 = (bf16[3,2,64,128]{3,2,1,0:T(8,128)(2,1)S(1)}, bf16[3,2,64,128]{3,2,1,0:T(8,128)(2,1)S(1)}, u32[]{:S(2)}, u32[]{:S(2)}) collective-permute-start(bf16[3,2,64,128]{3,2,1,0:T(8,128)(2,1)S(1)} %get-tuple-element.68), channel_id=1, source_target_pairs={{0,4},{4,0},{8,12},{12,8},{1,5},{5,1},{9,13},{13,9},{2,6},{6,2},{1... | collective-permute-start | bytes 294920 | tf_op jit(solution)/shard_map/ppermute | solution.py:18
  39.9 5.0 %collective-permute-start.16 = (bf16[3,2,64,128]{3,2,1,0:T(8,128)(2,1)S(1)}, bf16[3,2,64,128]{3,2,1,0:T(8,128)(2,1)S(1)}, u32[]{:S(2)}, u32[]{:S(2)}) collective-permute-start(bf16[3,2,64,128]{3,2,1,0:T(8,128)(2,1)S(1)} %get-tuple-element.69), channel_id=1, source_target_pairs={{0,4},{4,0},{8,12},{12,8},{1,5},{5,1},{9,13},{13,9},{2,6},{6,2},{1... | collective-permute-start | bytes 294920 | tf_op jit(solution)/shard_map/ppermute | solution.py:18
  40.4 7.3 %collective-permute-start.12 = (bf16[2,2,64,128]{3,2,1,0:T(8,128)(2,1)S(1)}, bf16[2,2,64,128]{3,2,1,0:T(8,128)(2,1)S(1)}, u32[]{:S(2)}, u32[]{:S(2)}) collective-permute-start(bf16[2,2,64,128]{3,2,1,0:T(8,128)(2,1)S(1)} %get-tuple-element.65), channel_id=1, source_target_pairs={{0,12},{4,8},{8,4},{12,0},{1,13},{5,9},{9,5},{13,1},{2,14},{6,10},... | collective-permute-start | bytes 196616 | tf_op jit(solution)/shard_map/ppermute | solution.py:18
  41.8 7.3 %collective-permute-start.14 = (bf16[2,2,64,128]{3,2,1,0:T(8,128)(2,1)S(1)}, bf16[2,2,64,128]{3,2,1,0:T(8,128)(2,1)S(1)}, u32[]{:S(2)}, u32[]{:S(2)}) collective-permute-start(bf16[2,2,64,128]{3,2,1,0:T(8,128)(2,1)S(1)} %get-tuple-element.67), channel_id=1, source_target_pairs={{0,12},{4,8},{8,4},{12,0},{1,13},{5,9},{9,5},{13,1},{2,14},{6,10},... | collective-permute-start | bytes 196616 | tf_op jit(solution)/shard_map/ppermute | solution.py:18
  44.3 7.9 %collective-permute-start.13 = (bf16[2,2,64,128]{3,2,1,0:T(8,128)(2,1)S(1)}, bf16[2,2,64,128]{3,2,1,0:T(8,128)(2,1)S(1)}, u32[]{:S(2)}, u32[]{:S(2)}) collective-permute-start(bf16[2,2,64,128]{3,2,1,0:T(8,128)(2,1)S(1)} %get-tuple-element.66.refs_3_), channel_id=1, source_target_pairs={{0,8},{4,12},{8,0},{12,4},{1,9},{5,13},{9,1},{13,5},{2,10},{6,14},... | collective-permute-start | bytes 196616 | tf_op jit(solution)/shard_map/ppermute | solution.py:18
  53.3 7.9 %collective-permute-start.18 = (bf16[256,1280]{1,0:T(8,128)(2,1)S(1)}, bf16[256,1280]{1,0:T(8,128)(2,1)S(1)}, u32[]{:S(2)}, u32[]{:S(2)}) collective-permute-start(bf16[256,1280]{1,0:T(8,128)(2,1)S(1)} %collective-permute-done.7.refs_2_), channel_id=1, source_target_pairs={{0,1},{1,0},{2,3},{3,2},{4,5},{5,4},{6,7},{7,6},{8,9},{9,8},{10,11... | collective-permute-start | bytes 1966088 | tf_op jit(solution)/shard_map/ppermute | solution.py:18

commit v3 on v2

--- a/solution.py
+++ b/solution.py
@@ -450,8 +450,7 @@
         ({m: pieces[m] for m in pieces if m}, loaded, output_weight)
     )
     pieces.update(far)
-    weights = {m: swap(output_weight, "rows", m) for m in (inner_size, 1)}
-    weights[0] = output_weight
+    weights = {0: output_weight, inner_size: swap(output_weight, "rows", inner_size)}
     pieces.update({m | 1: swap(piece, "rows", 1) for m, piece in pieces.items()})
     pieces = [pieces[m] for m in range(rows_size)]
     local_out = spatial_weight.shape[3]
@@ -467,8 +466,8 @@
     )
     first, second = neighbours(activated, "frames")
     send, chip_sum = spread(
-        [activated, first, second],
-        ((1, 1), (2, 0), (0, 2)),
+        [activated, second, first],
+        ((1, 1), (0, 2), (2, 0)),
         temporal_weight.reshape(3 * local_out, channels),
         outer_size,
         ("frames",),
@@ -504,11 +503,14 @@
             ]
         )
         pair_qkv.append(swap(sent[0], "frames", 1))
-    early, late = own_kv + far[0][:1], far[0][1:] + far[1]
-    state = attend(own_q, pair_qkv, early, (), not late)
-    own_out, pair_out = attend(own_q, pair_qkv, late, state, True) if late else state
+    turns = [own_kv + far[0][:1], far[0][1:] + far[1][1:], far[1][:1]]
+    turns = [kvs for kvs in turns if kvs]
+    state = ()
+    for turn, kvs in enumerate(turns):
+        state = attend(own_q, pair_qkv, kvs, state, turn == len(turns) - 1)
+    own_out, pair_out = state
     own_out, pair_out, weights = lax.optimization_barrier((own_out, pair_out, weights))
-    weights[inner_size + 1] = swap(weights[inner_size], "rows", 1)
+    weights.update({m | 1: swap(weight, "rows", 1) for m, weight in weights.items()})
     dealt = deal(own_out, pair_out, rows_size, "frames", "rows", inner_size)
     together = 2 * rows_size
     groups = [

time: 62.7 us -> 62.7 us (level)
  starting transfers between devices: 21.2 us -> 18.6 us
  waiting for transfers between devices: 20.1 us -> 22.3 us
    ppermute x2, starting transfers between devices: 5.13 us -> 2.3 us  [neighbours(): return (lax.ppermute(array, axis, even), lax.ppermute(array, axis, odd))]
    ppermute x17, waiting for transfers between devices: 15.7 us -> 18.2 us  [swap(): return lax.ppermute(array, axis, [(i, i ^ stride) for i in range(size)])]
    pallas_call x2 -> x3, Pallas kernels: 2.58 us -> 3.06 us  [attend(): pl.pallas_call(functools.partial(attention_kernel, parts=parts, kv_count=...]
  transfers between devices with their start and end apart: 19 -> 19, of which waited for: 10 -> 10; matrix products, arithmetic and copies ran while one was open for 0% -> 0% of each run, Pallas kernels for 12% -> 13%
where the time goes in v3:
time: 62.7 us; the launch traced here: 62.5 us
  waiting for transfers between devices  22.3 us (36%)
  starting transfers between devices  18.6 us (30%)
  Pallas kernels  10.5 us (17%)
  blocking collectives  7.74 us (12%)
  local copies, waits for them, and re-layouts  3.15 us (5%)
    ppermute x17, waiting for transfers between devices, swap(): return lax.ppermute(array, axis, [(i, i ^ stride) for i in range(size)])  18.2 us
    ppermute x17, starting transfers between devices, swap(): return lax.ppermute(array, axis, [(i, i ^ stride) for i in range(size)])  16.3 us
    all_to_all x1, blocking collectives, body(): lax.all_to_all(dealt.reshape((together,) + dealt.shape[2:]), ('frames', '...  7.74 us
    ppermute x2, waiting for transfers between devices, neighbours(): return (lax.ppermute(array, axis, even), lax.ppermute(array, axis, odd))  4.09 us
    unnamed x24, local copies, waits for them, and re-layouts  3.15 us
    pallas_call x3, Pallas kernels, attend(): pl.pallas_call(functools.partial(attention_kernel, parts=parts, kv_count=...  3.06 us
    pallas_call x1, Pallas kernels, conv_norm(): pl.pallas_call(functools.partial(conv_kernel, pieces=len(pieces), cols=co...  2.56 us
    ppermute x2, starting transfers between devices, neighbours(): return (lax.ppermute(array, axis, even), lax.ppermute(array, axis, odd))  2.3 us
  transfers between devices with their start and end apart: 19, of which 10 were waited for; matrix products, arithmetic and copies ran while one was open for 0% of the time, Pallas kernels for 13%

profile of v3, /device:TPU:0, one launch (start us, length us, event | category | flops | bytes accessed | tf_op | source)
XLA Modules:
  0.0 62.5 jit_solution(4851198196346111963)
XLA Ops:
  0.0 2.9 %collective-permute-start.1 = (bf16[64,1280]{1,0:T(8,128)(2,1)}, bf16[64,1280]{1,0:T(8,128)(2,1)S(1)}, u32[]{:S(2)}, u32[]{:S(2)}) collective-permute-start(bf16[64,1280]{1,0:T(8,128)(2,1)} %bitcast.11), channel_id=1, source_target_pairs={{0,2},{1,3},{2,0},{3,1},{4,6},{5,7},{6,4},{7,5},{8,10},{9,11},{10,... | collective-permute-start | bytes 491528 | tf_op jit(solution)/shard_map/ppermute | solution.py:18
  2.9 3.1 %copy-done.1 = bf16[3,3,1280,320]{2,3,1,0:T(8,128)(2,1)S(1)} copy-done((bf16[3,3,1280,320]{2,3,1,0:T(8,128)(2,1)S(1)}, bf16[3,3,1280,320]{2,3,1,0:T(8,128)(2,1)}, u32[]{:S(2)}) %copy-start.1) | copy-done | bytes 7372824
  6.1 0.6 shard_map.118.refs_4_
  6.7 0.7 %collective-permute-done.1.refs_2_.latents_ref = bf16[64,1280]{1,0:T(8,128)(2,1)S(1)} collective-permute-done((bf16[64,1280]{1,0:T(8,128)(2,1)}, bf16[64,1280]{1,0:T(8,128)(2,1)S(1)}, u32[]{:S(2)}, u32[]{:S(2)}) %collective-permute-start.1) | collective-permute-done | bytes 163872 | tf_op jit(solution)/shard_map/ppermute | solution.py:18
  7.4 1.7 %collective-permute-start.6 = (bf16[256,1280]{1,0:T(8,128)(2,1)S(1)}, bf16[256,1280]{1,0:T(8,128)(2,1)S(1)}, u32[]{:S(2)}, u32[]{:S(2)}) collective-permute-start(bf16[256,1280]{1,0:T(8,128)(2,1)S(1)} %copy-done.5), channel_id=1, source_target_pairs={{0,2},{1,3},{2,0},{3,1},{4,6},{5,7},{6,4},{7,5},{8,10},{9,11},{10,... | collective-permute-start | bytes 1966088 | tf_op jit(solution)/shard_map/ppermute | solution.py:18
  9.1 2.6 %shard_map.119.refs_0_ = bf16[320,256]{1,0:T(8,128)(2,1)S(1)} custom-call(bf16[64,1280]{1,0:T(8,128)(2,1)S(1)} %bitcast.13, bf16[64,1280]{1,0:T(8,128)(2,1)S(1)} %collective-permute-done.refs_1_, bf16[64,1280]{1,0:T(8,128)(2,1)S(1)} %collective-permute-done.1.refs_2_.latents_ref, bf16[64,1280]{1,0:T(8,128)(2,1)S(1)} %collective-permute-done.2.refs_3_, ...), custom_call_target="tpu_custom_call" | custom-call | flops 1887436800 | bytes 8192000 | tf_op jit(solution)/shard_map/pallas_call | solution.py:104
  11.7 1.6 %collective-permute-start.4 = (bf16[320,256]{1,0:T(8,128)(2,1)S(1)}, bf16[320,256]{1,0:T(8,128)(2,1)S(1)}, u32[]{:S(2)}, u32[]{:S(2)}) collective-permute-start(bf16[320,256]{1,0:T(8,128)(2,1)S(1)} %shard_map.119.refs_0_), channel_id=1, source_target_pairs={{0,4},{4,0},{8,12},{12,8},{1,5},{5,1},{9,13},{13,9},{2,6},{6,2},{1... | collective-permute-start | bytes 491528 | tf_op jit(solution)/shard_map/ppermute | solution.py:25
  13.3 0.7 %collective-permute-start.3 = (bf16[320,256]{1,0:T(8,128)(2,1)S(1)}, bf16[320,256]{1,0:T(8,128)(2,1)S(1)}, u32[]{:S(2)}, u32[]{:S(2)}) collective-permute-start(bf16[320,256]{1,0:T(8,128)(2,1)S(1)} %shard_map.119.refs_0_), channel_id=1, source_target_pairs={{4,8},{8,4},{5,9},{9,5},{6,10},{10,6},{7,11},{11,7},{20,24},{24,20... | collective-permute-start | bytes 491528 | tf_op jit(solution)/shard_map/ppermute | solution.py:25
  14.0 4.1 %collective-permute-done.4.refs_2_ = bf16[320,256]{1,0:T(8,128)(2,1)S(1)} collective-permute-done((bf16[320,256]{1,0:T(8,128)(2,1)S(1)}, bf16[320,256]{1,0:T(8,128)(2,1)S(1)}, u32[]{:S(2)}, u32[]{:S(2)}) %collective-permute-start.4) | collective-permute-done | bytes 163872 | tf_op jit(solution)/shard_map/ppermute | solution.py:25
  18.1 0.7 %shard_map.120 = (bf16[2,64,1280]{2,1,0:T(8,128)(2,1)S(1)}, bf16[2,64,960]{2,1,0:T(8,128)(2,1)S(1)}) custom-call(bf16[320,256]{1,0:T(8,128)(2,1)S(1)} %shard_map.119.refs_0_, bf16[320,256]{1,0:T(8,128)(2,1)S(1)} %collective-permute-done.3.refs_1_, bf16[320,256]{1,0:T(8,128)(2,1)S(1)} %collective-permute-done.4.refs_2_, bf16[960,1280]{1,0:T(8,128)(2,1)S(1)} %bitcast.8), custom_call_target="tpu_custom_call" | custom-call | flops 314572800 | bytes 3440640 | tf_op jit(solution)/shard_map/pallas_call | solution.py:158
  18.9 0.5 shard_map.121.mine_ref
  19.4 1.1 %collective-permute-done.5.theirs_ref = bf16[2,64,1280]{2,1,0:T(8,128)(2,1)S(1)} collective-permute-done((bf16[2,64,1280]{2,1,0:T(8,128)(2,1)S(1)}, bf16[2,64,1280]{2,1,0:T(8,128)(2,1)S(1)}, u32[]{:S(2)}, u32[]{:S(2)}) %collective-permute-start.5) | collective-permute-done | bytes 327712 | tf_op jit(solution)/shard_map/ppermute | solution.py:18
  20.6 3.9 %collective-permute-done.6.refs_2_ = bf16[256,1280]{1,0:T(8,128)(2,1)S(1)} collective-permute-done((bf16[256,1280]{1,0:T(8,128)(2,1)S(1)}, bf16[256,1280]{1,0:T(8,128)(2,1)S(1)}, u32[]{:S(2)}, u32[]{:S(2)}) %collective-permute-start.6) | collective-permute-done | bytes 655392 | tf_op jit(solution)/shard_map/ppermute | solution.py:18
  24.5 1.7 %collective-permute-start.7 = (bf16[64,1280]{1,0:T(8,128)(2,1)S(1)}, bf16[64,1280]{1,0:T(8,128)(2,1)S(1)}, u32[]{:S(2)}, u32[]{:S(2)}) collective-permute-start(bf16[64,1280]{1,0:T(8,128)(2,1)S(1)} %get-tuple-element.55), channel_id=1, source_target_pairs={{0,2},{1,3},{2,0},{3,1},{4,6},{5,7},{6,4},{7,5},{8,10},{9,11},{10,... | collective-permute-start | bytes 491528 | tf_op jit(solution)/shard_map/ppermute | solution.py:18
  26.5 5.1 %collective-permute-done.7.theirs_ref = bf16[64,1280]{1,0:T(8,128)(2,1)S(1)} collective-permute-done((bf16[64,1280]{1,0:T(8,128)(2,1)S(1)}, bf16[64,1280]{1,0:T(8,128)(2,1)S(1)}, u32[]{:S(2)}, u32[]{:S(2)}) %collective-permute-start.7) | collective-permute-done | bytes 163872 | tf_op jit(solution)/shard_map/ppermute | solution.py:18
  32.0 1.9 %collective-permute-done.9.theirs_ref = bf16[64,1280]{1,0:T(8,128)(2,1)S(1)} collective-permute-done((bf16[64,1280]{1,0:T(8,128)(2,1)S(1)}, bf16[64,1280]{1,0:T(8,128)(2,1)S(1)}, u32[]{:S(2)}, u32[]{:S(2)}) %collective-permute-start.9) | collective-permute-done | bytes 163872 | tf_op jit(solution)/shard_map/ppermute | solution.py:18
  34.2 0.6 shard_map.124
  34.8 2.9 %collective-permute-start.16 = (bf16[2,2,64,128]{3,2,1,0:T(8,128)(2,1)S(1)}, bf16[2,2,64,128]{3,2,1,0:T(8,128)(2,1)S(1)}, u32[]{:S(2)}, u32[]{:S(2)}) collective-permute-start(bf16[2,2,64,128]{3,2,1,0:T(8,128)(2,1)S(1)} %get-tuple-element.71.refs_2_), channel_id=1, source_target_pairs={{0,8},{4,12},{8,0},{12,4},{1,9},{5,13},{9,1},{13,5},{2,10},{6,14},... | collective-permute-start | bytes 196616 | tf_op jit(solution)/shard_map/ppermute | solution.py:18
  37.7 1.6 %collective-permute-start.12 = (bf16[3,2,64,128]{3,2,1,0:T(8,128)(2,1)S(1)}, bf16[3,2,64,128]{3,2,1,0:T(8,128)(2,1)S(1)}, u32[]{:S(2)}, u32[]{:S(2)}) collective-permute-start(bf16[3,2,64,128]{3,2,1,0:T(8,128)(2,1)S(1)} %get-tuple-element.67), channel_id=1, source_target_pairs={{0,4},{4,0},{8,12},{12,8},{1,5},{5,1},{9,13},{13,9},{2,6},{6,2},{1... | collective-permute-start | bytes 294920 | tf_op jit(solution)/shard_map/ppermute | solution.py:18
  39.3 0.6 shard_map.126
  39.9 0.5 collective-permute-start.13
  40.4 1.3 %collective-permute-start.14 = (bf16[2,2,64,128]{3,2,1,0:T(8,128)(2,1)S(1)}, bf16[2,2,64,128]{3,2,1,0:T(8,128)(2,1)S(1)}, u32[]{:S(2)}, u32[]{:S(2)}) collective-permute-start(bf16[2,2,64,128]{3,2,1,0:T(8,128)(2,1)S(1)} %get-tuple-element.69), channel_id=1, source_target_pairs={{0,12},{4,8},{8,4},{12,0},{1,13},{5,9},{9,5},{13,1},{2,14},{6,10},... | collective-permute-start | bytes 196616 | tf_op jit(solution)/shard_map/ppermute | solution.py:18
  41.8 2.5 %collective-permute-start.15 = (bf16[2,2,64,128]{3,2,1,0:T(8,128)(2,1)S(1)}, bf16[2,2,64,128]{3,2,1,0:T(8,128)(2,1)S(1)}, u32[]{:S(2)}, u32[]{:S(2)}) collective-permute-start(bf16[2,2,64,128]{3,2,1,0:T(8,128)(2,1)S(1)} %get-tuple-element.70), channel_id=1, source_target_pairs={{0,12},{4,8},{8,4},{12,0},{1,13},{5,9},{9,5},{13,1},{2,14},{6,10},... | collective-permute-start | bytes 196616 | tf_op jit(solution)/shard_map/ppermute | solution.py:18
  44.3 0.7 %collective-permute-done.13.refs_6_.refs_5_.refs_4_ = bf16[3,2,64,128]{3,2,1,0:T(8,128)(2,1)S(1)} collective-permute-done((bf16[3,2,64,128]{3,2,1,0:T(8,128)(2,1)S(1)}, bf16[3,2,64,128]{3,2,1,0:T(8,128)(2,1)S(1)}, u32[]{:S(2)}, u32[]{:S(2)}) %collective-permute-start.13) | collective-permute-done | bytes 98336 | tf_op jit(solution)/shard_map/ppermute | solution.py:18
  45.0 1.4 %shard_map.127 = (f32[2,1,512]{2,1,0:T(1,128)S(1)}, f32[2,1,512]{2,1,0:T(1,128)S(1)}, f32[2,64,512]{2,1,0:T(8,128)S(1)}) custom-call(bf16[2,64,128]{2,1,0:T(8,128)(2,1)S(1)} %get-tuple-element.62.refs_0_, bf16[2,64,128]{2,1,0:T(8,128)(2,1)S(1)} %get-tuple-element.65.refs_1_, bf16[2,2,64,128]{3,2,1,0:T(8,128)(2,1)S(1)} %get-tuple-element.71.refs_2_, ...), custom_call_target="tpu_custom_call" | custom-call | flops 167772160 | bytes 458752 | tf_op jit(solution)/shard_map/pallas_call | solution.py:406
  46.4 1.3 %collective-permute-done.14.refs_2_ = bf16[2,2,64,128]{3,2,1,0:T(8,128)(2,1)S(1)} collective-permute-done((bf16[2,2,64,128]{3,2,1,0:T(8,128)(2,1)S(1)}, bf16[2,2,64,128]{3,2,1,0:T(8,128)(2,1)S(1)}, u32[]{:S(2)}, u32[]{:S(2)}) %collective-permute-start.14) | collective-permute-done | bytes 65568 | tf_op jit(solution)/shard_map/ppermute | solution.py:18
  47.7 1.4 %collective-permute-done.15.refs_3_ = bf16[2,2,64,128]{3,2,1,0:T(8,128)(2,1)S(1)} collective-permute-done((bf16[2,2,64,128]{3,2,1,0:T(8,128)(2,1)S(1)}, bf16[2,2,64,128]{3,2,1,0:T(8,128)(2,1)S(1)}, u32[]{:S(2)}, u32[]{:S(2)}) %collective-permute-start.15) | collective-permute-done | bytes 65568 | tf_op jit(solution)/shard_map/ppermute | solution.py:18
  49.1 0.8 %shard_map.128 = (f32[2,1,512]{2,1,0:T(1,128)S(1)}, f32[2,1,512]{2,1,0:T(1,128)S(1)}, f32[2,64,512]{2,1,0:T(8,128)S(1)}) custom-call(bf16[2,64,128]{2,1,0:T(8,128)(2,1)S(1)} %get-tuple-element.62.refs_0_, bf16[2,64,128]{2,1,0:T(8,128)(2,1)S(1)} %get-tuple-element.65.refs_1_, bf16[2,2,64,128]{3,2,1,0:T(8,128)(2,1)S(1)} %collective-permute-done.14.refs_2_, ...), custom_call_target="tpu_custom_call" | custom-call | flops 67108864 | bytes 663552 | tf_op jit(solution)/shard_map/pallas_call | solution.py:406
  50.0 2.2 %collective-permute-done.11.refs_2_ = bf16[2,2,64,128]{3,2,1,0:T(8,128)(2,1)S(1)} collective-permute-done((bf16[2,2,64,128]{3,2,1,0:T(8,128)(2,1)S(1)}, bf16[2,2,64,128]{3,2,1,0:T(8,128)(2,1)S(1)}, u32[]{:S(2)}, u32[]{:S(2)}) %collective-permute-start.11) | collective-permute-done | bytes 65568 | tf_op jit(solution)/shard_map/ppermute | solution.py:18
  52.1 0.8 %shard_map.129 = (bf16[256,128]{1,0:T(8,128)(2,1)S(1)}, bf16[256,128]{1,0:T(8,128)(2,1)S(1)}) custom-call(bf16[2,64,128]{2,1,0:T(8,128)(2,1)S(1)} %get-tuple-element.62.refs_0_, bf16[2,64,128]{2,1,0:T(8,128)(2,1)S(1)} %get-tuple-element.65.refs_1_, bf16[2,2,64,128]{3,2,1,0:T(8,128)(2,1)S(1)} %collective-permute-done.11.refs_2_, ...), custom_call_target="tpu_custom_call" | custom-call | flops 33554432 | bytes 598016 | tf_op jit(solution)/shard_map/pallas_call | solution.py:406
  53.6 7.7 %all_to_all.5 = bf16[8,64,128]{2,1,0:T(8,128)(2,1)S(1)} all-to-all(bf16[8,64,128]{2,1,0:T(8,128)(2,1)S(1)} %bitcast.16), channel_id=1, replica_groups={{0,1,2,3,4,5,6,7},{8,9,10,11,12,13,14,15},{16,17,18,19,20,21,22,23},{24..., dimensions={0} | all-to-all | bytes 262144 | tf_op jit(solution)/shard_map/all_to_all | solution.py:520
  61.3 1.2 %shard_map.131 = bf16[64,1280]{1,0:T(8,128)(2,1)} custom-call(bf16[2,4,64,128]{3,2,1,0:T(8,128)(2,1)S(1)} %bitcast.15, bf16[256,1280]{1,0:T(8,128)(2,1)S(1)} %copy-done.5, bf16[256,1280]{1,0:T(8,128)(2,1)S(1)} %collective-permute-done.17.refs_1_, bf16[256,1280]{1,0:T(8,128)(2,1)S(1)} %collective-permute-done.6.refs_2_, ...), custom_call_target="tpu_custom_call" | custom-call | flops 167772160 | bytes 2949120 | tf_op jit(solution)/shard_map/pallas_call | solution.py:250
  (45 shorter events, 1.8 us)
Async XLA Ops:
  0.0 7.3 %collective-permute-start.1 = (bf16[64,1280]{1,0:T(8,128)(2,1)}, bf16[64,1280]{1,0:T(8,128)(2,1)S(1)}, u32[]{:S(2)}, u32[]{:S(2)}) collective-permute-start(bf16[64,1280]{1,0:T(8,128)(2,1)} %bitcast.11), channel_id=1, source_target_pairs={{0,2},{1,3},{2,0},{3,1},{4,6},{5,7},{6,4},{7,5},{8,10},{9,11},{10,... | collective-permute-start | bytes 491528 | tf_op jit(solution)/shard_map/ppermute | solution.py:18
  2.9 6.2 %collective-permute-start = (bf16[64,1280]{1,0:T(8,128)(2,1)}, bf16[64,1280]{1,0:T(8,128)(2,1)S(1)}, u32[]{:S(2)}, u32[]{:S(2)}) collective-permute-start(bf16[64,1280]{1,0:T(8,128)(2,1)} %bitcast.12), channel_id=1, source_target_pairs={{0,1},{1,0},{2,3},{3,2},{4,5},{5,4},{6,7},{7,6},{8,9},{9,8},{10,11... | collective-permute-start | bytes 491528 | tf_op jit(solution)/shard_map/ppermute | solution.py:18
  2.9 3.1 %copy-start.1 = (bf16[3,3,1280,320]{2,3,1,0:T(8,128)(2,1)S(1)}, bf16[3,3,1280,320]{2,3,1,0:T(8,128)(2,1)}, u32[]{:S(2)}) copy-start(bf16[3,3,1280,320]{2,3,1,0:T(8,128)(2,1)} %param.13) | copy-start | bytes 22118404
  6.0 1.3 %copy-start.5 = (bf16[256,1280]{1,0:T(8,128)(2,1)S(1)}, bf16[256,1280]{1,0:T(8,128)(2,1)}, u32[]{:S(2)}) copy-start(bf16[256,1280]{1,0:T(8,128)(2,1)} %refs_0_) | copy-start | bytes 1966084
  6.0 3.1 %copy-start.6 = (bf16[4,1,16,1280]{3,2,1,0:T(8,128)(2,1)S(1)}, bf16[4,1,16,1280]{3,2,1,0:T(8,128)(2,1)}, u32[]{:S(2)}) copy-start(bf16[4,1,16,1280]{3,2,1,0:T(8,128)(2,1)} %param.12) | copy-start | bytes 491524
  6.0 3.1 %copy-start.9 = (f32[320]{0:T(512)S(1)}, f32[320]{0:T(512)}, u32[]{:S(2)}) copy-start(f32[320]{0:T(512)} %refs_5_.1) | copy-start | bytes 3844
  6.0 3.1 %copy-start.10 = (f32[320]{0:T(512)S(1)}, f32[320]{0:T(512)}, u32[]{:S(2)}) copy-start(f32[320]{0:T(512)} %refs_6_.1) | copy-start | bytes 3844
  6.0 3.1 %copy-start.11 = (f32[320]{0:T(512)S(1)}, f32[320]{0:T(512)}, u32[]{:S(2)}) copy-start(f32[320]{0:T(512)} %refs_7_.1) | copy-start | bytes 3844
  6.6 11.5 %copy-start = (bf16[3,320,1280]{2,1,0:T(8,128)(2,1)S(1)}, bf16[3,320,1280]{2,1,0:T(8,128)(2,1)}, u32[]{:S(2)}) copy-start(bf16[3,320,1280]{2,1,0:T(8,128)(2,1)} %param.17) | copy-start | bytes 7372804
  6.6 25.0 %copy-start.7 = (f32[1280]{0:T(1024)S(1)}, f32[1280]{0:T(1024)}, u32[]{:S(2)}) copy-start(f32[1280]{0:T(1024)} %bias_ref.3) | copy-start | bytes 15364
  6.6 25.0 %copy-start.8 = (f32[1280]{0:T(1024)S(1)}, f32[1280]{0:T(1024)}, u32[]{:S(2)}) copy-start(f32[1280]{0:T(1024)} %gain_ref.3) | copy-start | bytes 15364
  6.7 27.6 %copy-start.2 = (bf16[1280,256]{1,0:T(8,128)(2,1)S(1)}, bf16[1280,256]{1,0:T(8,128)(2,1)}, u32[]{:S(2)}) copy-start(bf16[1280,256]{1,0:T(8,128)(2,1)} %refs_2_.3) | copy-start | bytes 1966084
  6.7 27.5 %copy-start.3 = (bf16[1280,256]{1,0:T(8,128)(2,1)S(1)}, bf16[1280,256]{1,0:T(8,128)(2,1)}, u32[]{:S(2)}) copy-start(bf16[1280,256]{1,0:T(8,128)(2,1)} %refs_3_.3) | copy-start | bytes 1966084
  6.7 27.5 %copy-start.4 = (bf16[1280,256]{1,0:T(8,128)(2,1)S(1)}, bf16[1280,256]{1,0:T(8,128)(2,1)}, u32[]{:S(2)}) copy-start(bf16[1280,256]{1,0:T(8,128)(2,1)} %refs_4_.3) | copy-start | bytes 1966084
  7.3 1.8 %collective-permute-start.2 = (bf16[64,1280]{1,0:T(8,128)(2,1)S(1)}, bf16[64,1280]{1,0:T(8,128)(2,1)S(1)}, u32[]{:S(2)}, u32[]{:S(2)}) collective-permute-start(bf16[64,1280]{1,0:T(8,128)(2,1)S(1)} %collective-permute-done.1.refs_2_.latents_ref), channel_id=1, source_target_pairs={{0,1},{1,0},{2,3},{3,2},{4,5},{5,4},{6,7},{7,6},{8,9},{9,8},{10,11... | collective-permute-start | bytes 491528 | tf_op jit(solution)/shard_map/ppermute | solution.py:18
  7.4 17.1 %collective-permute-start.6 = (bf16[256,1280]{1,0:T(8,128)(2,1)S(1)}, bf16[256,1280]{1,0:T(8,128)(2,1)S(1)}, u32[]{:S(2)}, u32[]{:S(2)}) collective-permute-start(bf16[256,1280]{1,0:T(8,128)(2,1)S(1)} %copy-done.5), channel_id=1, source_target_pairs={{0,2},{1,3},{2,0},{3,1},{4,6},{5,7},{6,4},{7,5},{8,10},{9,11},{10,... | collective-permute-start | bytes 1966088 | tf_op jit(solution)/shard_map/ppermute | solution.py:18
  11.7 6.4 %collective-permute-start.4 = (bf16[320,256]{1,0:T(8,128)(2,1)S(1)}, bf16[320,256]{1,0:T(8,128)(2,1)S(1)}, u32[]{:S(2)}, u32[]{:S(2)}) collective-permute-start(bf16[320,256]{1,0:T(8,128)(2,1)S(1)} %shard_map.119.refs_0_), channel_id=1, source_target_pairs={{0,4},{4,0},{8,12},{12,8},{1,5},{5,1},{9,13},{13,9},{2,6},{6,2},{1... | collective-permute-start | bytes 491528 | tf_op jit(solution)/shard_map/ppermute | solution.py:25
  13.3 4.8 %collective-permute-start.3 = (bf16[320,256]{1,0:T(8,128)(2,1)S(1)}, bf16[320,256]{1,0:T(8,128)(2,1)S(1)}, u32[]{:S(2)}, u32[]{:S(2)}) collective-permute-start(bf16[320,256]{1,0:T(8,128)(2,1)S(1)} %shard_map.119.refs_0_), channel_id=1, source_target_pairs={{4,8},{8,4},{5,9},{9,5},{6,10},{10,6},{7,11},{11,7},{20,24},{24,20... | collective-permute-start | bytes 491528 | tf_op jit(solution)/shard_map/ppermute | solution.py:25
  18.8 1.7 %collective-permute-start.5 = (bf16[2,64,1280]{2,1,0:T(8,128)(2,1)S(1)}, bf16[2,64,1280]{2,1,0:T(8,128)(2,1)S(1)}, u32[]{:S(2)}, u32[]{:S(2)}) collective-permute-start(bf16[2,64,1280]{2,1,0:T(8,128)(2,1)S(1)} %get-tuple-element.50), channel_id=1, source_target_pairs={{0,1},{1,0},{2,3},{3,2},{4,5},{5,4},{6,7},{7,6},{8,9},{9,8},{10,11... | collective-permute-start | bytes 983048 | tf_op jit(solution)/shard_map/ppermute | solution.py:18
  24.5 7.1 %collective-permute-start.7 = (bf16[64,1280]{1,0:T(8,128)(2,1)S(1)}, bf16[64,1280]{1,0:T(8,128)(2,1)S(1)}, u32[]{:S(2)}, u32[]{:S(2)}) collective-permute-start(bf16[64,1280]{1,0:T(8,128)(2,1)S(1)} %get-tuple-element.55), channel_id=1, source_target_pairs={{0,2},{1,3},{2,0},{3,1},{4,6},{5,7},{6,4},{7,5},{8,10},{9,11},{10,... | collective-permute-start | bytes 491528 | tf_op jit(solution)/shard_map/ppermute | solution.py:18
  26.2 7.6 %collective-permute-start.9 = (bf16[64,1280]{1,0:T(8,128)(2,1)S(1)}, bf16[64,1280]{1,0:T(8,128)(2,1)S(1)}, u32[]{:S(2)}, u32[]{:S(2)}) collective-permute-start(bf16[64,1280]{1,0:T(8,128)(2,1)S(1)} %get-tuple-element.57), channel_id=1, source_target_pairs={{0,2},{1,3},{2,0},{3,1},{4,6},{5,7},{6,4},{7,5},{8,10},{9,11},{10,... | collective-permute-start | bytes 491528 | tf_op jit(solution)/shard_map/ppermute | solution.py:18
  31.9 2.0 %collective-permute-start.8 = (bf16[64,1280]{1,0:T(8,128)(2,1)S(1)}, bf16[64,1280]{1,0:T(8,128)(2,1)S(1)}, u32[]{:S(2)}, u32[]{:S(2)}) collective-permute-start(bf16[64,1280]{1,0:T(8,128)(2,1)S(1)} %get-tuple-element.60.refs_0_), channel_id=1, source_target_pairs={{0,1},{1,0},{2,3},{3,2},{4,5},{5,4},{6,7},{7,6},{8,9},{9,8},{10,11... | collective-permute-start | bytes 491528 | tf_op jit(solution)/shard_map/ppermute | solution.py:18
  34.1 5.2 %collective-permute-start.10 = (bf16[64,1280]{1,0:T(8,128)(2,1)S(1)}, bf16[64,1280]{1,0:T(8,128)(2,1)S(1)}, u32[]{:S(2)}, u32[]{:S(2)}) collective-permute-start(bf16[64,1280]{1,0:T(8,128)(2,1)S(1)} %shard_map.125.refs_0_), channel_id=1, source_target_pairs={{0,1},{1,0},{2,3},{3,2},{4,5},{5,4},{6,7},{7,6},{8,9},{9,8},{10,11... | collective-permute-start | bytes 491528 | tf_op jit(solution)/shard_map/ppermute | solution.py:18
  34.8 9.4 %collective-permute-start.16 = (bf16[2,2,64,128]{3,2,1,0:T(8,128)(2,1)S(1)}, bf16[2,2,64,128]{3,2,1,0:T(8,128)(2,1)S(1)}, u32[]{:S(2)}, u32[]{:S(2)}) collective-permute-start(bf16[2,2,64,128]{3,2,1,0:T(8,128)(2,1)S(1)} %get-tuple-element.71.refs_2_), channel_id=1, source_target_pairs={{0,8},{4,12},{8,0},{12,4},{1,9},{5,13},{9,1},{13,5},{2,10},{6,14},... | collective-permute-start | bytes 196616 | tf_op jit(solution)/shard_map/ppermute | solution.py:18
  37.7 6.5 %collective-permute-start.12 = (bf16[3,2,64,128]{3,2,1,0:T(8,128)(2,1)S(1)}, bf16[3,2,64,128]{3,2,1,0:T(8,128)(2,1)S(1)}, u32[]{:S(2)}, u32[]{:S(2)}) collective-permute-start(bf16[3,2,64,128]{3,2,1,0:T(8,128)(2,1)S(1)} %get-tuple-element.67), channel_id=1, source_target_pairs={{0,4},{4,0},{8,12},{12,8},{1,5},{5,1},{9,13},{13,9},{2,6},{6,2},{1... | collective-permute-start | bytes 294920 | tf_op jit(solution)/shard_map/ppermute | solution.py:18
  39.9 5.0 %collective-permute-start.13 = (bf16[3,2,64,128]{3,2,1,0:T(8,128)(2,1)S(1)}, bf16[3,2,64,128]{3,2,1,0:T(8,128)(2,1)S(1)}, u32[]{:S(2)}, u32[]{:S(2)}) collective-permute-start(bf16[3,2,64,128]{3,2,1,0:T(8,128)(2,1)S(1)} %get-tuple-element.68), channel_id=1, source_target_pairs={{0,4},{4,0},{8,12},{12,8},{1,5},{5,1},{9,13},{13,9},{2,6},{6,2},{1... | collective-permute-start | bytes 294920 | tf_op jit(solution)/shard_map/ppermute | solution.py:18
  40.4 7.3 %collective-permute-start.14 = (bf16[2,2,64,128]{3,2,1,0:T(8,128)(2,1)S(1)}, bf16[2,2,64,128]{3,2,1,0:T(8,128)(2,1)S(1)}, u32[]{:S(2)}, u32[]{:S(2)}) collective-permute-start(bf16[2,2,64,128]{3,2,1,0:T(8,128)(2,1)S(1)} %get-tuple-element.69), channel_id=1, source_target_pairs={{0,12},{4,8},{8,4},{12,0},{1,13},{5,9},{9,5},{13,1},{2,14},{6,10},... | collective-permute-start | bytes 196616 | tf_op jit(solution)/shard_map/ppermute | solution.py:18
  41.8 7.3 %collective-permute-start.15 = (bf16[2,2,64,128]{3,2,1,0:T(8,128)(2,1)S(1)}, bf16[2,2,64,128]{3,2,1,0:T(8,128)(2,1)S(1)}, u32[]{:S(2)}, u32[]{:S(2)}) collective-permute-start(bf16[2,2,64,128]{3,2,1,0:T(8,128)(2,1)S(1)} %get-tuple-element.70), channel_id=1, source_target_pairs={{0,12},{4,8},{8,4},{12,0},{1,13},{5,9},{9,5},{13,1},{2,14},{6,10},... | collective-permute-start | bytes 196616 | tf_op jit(solution)/shard_map/ppermute | solution.py:18
  44.3 7.9 %collective-permute-start.11 = (bf16[2,2,64,128]{3,2,1,0:T(8,128)(2,1)S(1)}, bf16[2,2,64,128]{3,2,1,0:T(8,128)(2,1)S(1)}, u32[]{:S(2)}, u32[]{:S(2)}) collective-permute-start(bf16[2,2,64,128]{3,2,1,0:T(8,128)(2,1)S(1)} %get-tuple-element.66.refs_3_), channel_id=1, source_target_pairs={{0,8},{4,12},{8,0},{12,4},{1,9},{5,13},{9,1},{13,5},{2,10},{6,14},... | collective-permute-start | bytes 196616 | tf_op jit(solution)/shard_map/ppermute | solution.py:18
  53.0 8.3 %collective-permute-start.17 = (bf16[256,1280]{1,0:T(8,128)(2,1)S(1)}, bf16[256,1280]{1,0:T(8,128)(2,1)S(1)}, u32[]{:S(2)}, u32[]{:S(2)}) collective-permute-start(bf16[256,1280]{1,0:T(8,128)(2,1)S(1)} %copy-done.5), channel_id=1, source_target_pairs={{0,1},{1,0},{2,3},{3,2},{4,5},{5,4},{6,7},{7,6},{8,9},{9,8},{10,11... | collective-permute-start | bytes 1966088 | tf_op jit(solution)/shard_map/ppermute | solution.py:18
  53.0 8.3 %collective-permute-start.18 = (bf16[256,1280]{1,0:T(8,128)(2,1)S(1)}, bf16[256,1280]{1,0:T(8,128)(2,1)S(1)}, u32[]{:S(2)}, u32[]{:S(2)}) collective-permute-start(bf16[256,1280]{1,0:T(8,128)(2,1)S(1)} %collective-permute-done.6.refs_2_), channel_id=1, source_target_pairs={{0,1},{1,0},{2,3},{3,2},{4,5},{5,4},{6,7},{7,6},{8,9},{9,8},{10,11... | collective-permute-start | bytes 1966088 | tf_op jit(solution)/shard_map/ppermute | solution.py:18
